TPU v7x, 32 devices: a whole 2x2x4 slice. The times are simulated.
32 devices in a mesh: row: 4 (over z), col: 8 (over y, x, core).
Axes of the slice: x: 2, y: 2, z: 4, core: 2. Of those that a mesh axis runs over, the one named last changes fastest.
Arguments:
- spectra: bfloat16 [6144, 144, 128], P(('row', 'col')), may hold values from -30 to 30
- station_ids: int32 [6144], P(('row', 'col')), may hold values from 0 to 3071, as said below
- counts: int32 [32], P(('row', 'col')), may hold values from 0 to 192, as said below
Outputs:
- cross_spectra: bfloat16 [3, 2, 3072, 3072], P(None, None, 'row', 'col')
Inputs may be any that keep to these rules, and one draw needn't show every extreme that they name: `station_ids`: the live slots of all readers name every station exactly once; slots at or past a reader's count hold arbitrary station numbers and carry no data. The counts sum to 3072. Among the live slots of one reader, at most 6 name stations of one block h * 96 to h * 96 + 95, and that number is reached in every draw.
All inputs are finite; a program needn't handle non-finite values.
Results may differ from a plain program's by a relative error of at most 0.001.
Values may be sent and summed in bfloat16 or wider, within the bound.
No kernel may reach another device: no remote copies, remote signals or barrier semaphores. Data moves between devices by JAX's collectives and lax.ppermute only.
A program may use at most 128 MiB of HBM per device.

v0:
```python
import math

import jax
import jax.numpy as jnp
from jax import lax
from jax.sharding import PartitionSpec as P

power_floor = 0.25


def whiten(raw):
    values = raw.astype(jnp.float32)
    band = values.shape[2] // 2
    real_part = values[:, :, :band]
    imag_part = values[:, :, band:]
    energy = real_part * real_part + imag_part * imag_part
    pieces = []
    for bin_index in range(3):
        lower = bin_index * band // 4
        averaged = jnp.mean(energy[:, :, lower : lower + band // 2], axis=2)
        amplitude = jnp.sqrt(jnp.maximum(averaged, power_floor))
        center = lower + band // 4
        pieces.append(real_part[:, :, center] / amplitude)
        pieces.append(imag_part[:, :, center] / amplitude)
    return jnp.concatenate(pieces, axis=1)


def pack_slots(payload, flat_index, total_slots, per_peer, readers):
    blank_rows = jnp.zeros((total_slots,) + payload.shape[1:], payload.dtype)
    filled = blank_rows.at[flat_index].set(payload, mode="drop")
    return filled.reshape((readers, per_peer) + payload.shape[1:])


def settle(received, received_ids, first_station, home_rows):
    flat_ids = received_ids.reshape(-1)
    flat_rows = received.reshape((flat_ids.shape[0],) + received.shape[2:])
    position = jnp.where(flat_ids >= 0, flat_ids - first_station, home_rows)
    blank_rows = jnp.zeros((home_rows,) + received.shape[2:], received.dtype)
    return blank_rows.at[position].set(flat_rows, mode="drop")


def pair_tile(row_part, column_part):
    segments = row_part.shape[1] // 6
    norm_factor = 1.0 / math.sqrt(segments)
    row_total = row_part.shape[0]
    column_total = column_part.shape[0]
    tiles = []
    for bin_index in range(3):
        real_imag = row_part[:, bin_index * 2 * segments : (bin_index + 1) * 2 * segments]
        rotated = jnp.concatenate([real_imag[:, segments:], -real_imag[:, :segments]], axis=1)
        stacked = jnp.concatenate([real_imag, rotated], axis=0)
        other = column_part[:, bin_index * 2 * segments : (bin_index + 1) * 2 * segments]
        product = lax.dot_general(
            stacked,
            other,
            (((1,), (1,)), ((), ())),
            precision=lax.Precision.HIGHEST,
            preferred_element_type=jnp.float32,
        )
        tiles.append(
            (product * norm_factor).astype(jnp.bfloat16).reshape(2, row_total, column_total)
        )
    return jnp.stack(tiles, axis=0)


def shards(spectra, station_ids, counts):
    row_count = lax.axis_size("row")
    column_count = lax.axis_size("col")
    readers = row_count * column_count
    slot_count = spectra.shape[0]
    home_rows = slot_count // 2
    per_peer = 2 * ((home_rows + readers - 1) // readers)
    total_slots = readers * per_peer
    target = station_ids // home_rows
    is_live = jnp.arange(slot_count, dtype=jnp.int32) < counts[0]
    matches = (target[:, None] == jnp.arange(readers, dtype=jnp.int32)[None, :]) & is_live[:, None]
    matches = matches.astype(jnp.int32)
    earlier = jnp.cumsum(matches, axis=0) - matches
    within = jnp.sum(earlier * matches, axis=1)
    flat_index = jnp.where(is_live, target * per_peer + within, total_slots)
    labels = jnp.full((total_slots,), -1, jnp.int32).at[flat_index].set(station_ids, mode="drop")
    labels = labels.reshape(readers, per_peer)
    first_station = (lax.axis_index("row") * column_count + lax.axis_index("col")) * home_rows
    ready = whiten(spectra)
    packed = pack_slots(ready, flat_index, total_slots, per_peer, readers)
    received, received_ids = (
        lax.all_to_all(packed, ("row", "col"), split_axis=0, concat_axis=0, tiled=True),
        lax.all_to_all(labels, ("row", "col"), split_axis=0, concat_axis=0, tiled=True),
    )
    white = settle(received, received_ids, first_station, home_rows)
    row_stations = lax.all_gather(white, "col", axis=0, tiled=True)
    return pair_tile(row_stations, lax.all_gather(white, "row", axis=0, tiled=True))


def solution(mesh):
    in_specs = (P(("row", "col"), None, None), P(("row", "col")), P(("row", "col")))
    out_specs = P(None, None, "row", "col")
    return jax.shard_map(shards, mesh=mesh, in_specs=in_specs, out_specs=out_specs, check_vma=False)
```

profile of v0, /device:TPU:0, one launch (start us, length us, event | category | flops | bytes accessed | tf_op | source)
XLA Modules:
  0.0 194.2 jit_solution(18023651555386337264)
XLA Ops:
  9.6 1.4 scatter_custom_fusion
  11.6 7.3 %all-to-all-start = ((s32[32,1,6]{2,1,0:T(1,128)}), s32[32,1,6]{2,1,0:T(1,128)S(1)}, u32[]{:S(2)}, u32[]{:S(2)}) async-start(s32[32,1,6]{2,1,0:T(1,128)} %bitcast.2), calls=%async_computation | async-start | bytes 32768 | tf_op jit(solution)/shard_map/all_to_all | solution.py:88
  18.9 13.6 %copy.19 = bf16[192,144,128]{0,1,2:T(8,128)(2,1)} copy(bf16[192,144,128]{2,1,0:T(8,128)(2,1)} %param.3) | data formatting | bytes 14155776 | tf_op args[0]
  32.6 12.9 %convert_element_type.17 = f32[192,144,128]{0,1,2:T(8,128)} convert(bf16[192,144,128]{0,1,2:T(8,128)(2,1)} %copy.19) | non-fusion elementwise | flops 3538944 | bytes 21233664 | tf_op jit(solution)/shard_map/convert_element_type | solution.py:12
  45.4 12.0 %fusion = f32[192,144,64]{0,1,2:T(8,128)} fusion(f32[192,144,128]{0,1,2:T(8,128)} %convert_element_type.17), kind=kLoop, calls=%fused_computation.4 | loop fusion | flops 5308416 | bytes 21233664 | tf_op jit(solution)/shard_map/add | solution.py:16
  57.4 6.4 %slice_reduce_fusion = (f32[192,144]{0,1:T(8,128)S(1)}, f32[192,144]{0,1:T(8,128)S(1)}, f32[192,144]{0,1:T(8,128)S(1)}) fusion(f32[192,144,64]{0,1,2:T(8,128)} %fusion), kind=kLoop, calls=%fused_computation.6 | loop fusion | flops 2571264 | bytes 10948608 | tf_op jit(solution)/shard_map/reduce_sum | solution.py:20
  63.8 1.0 fusion.37
  64.8 1.0 fusion.35
  65.8 1.0 fusion.33
  66.8 1.0 fusion.31
  67.7 1.0 fusion.29
  70.0 1.4 scatter_custom_fusion.1
  71.4 1.0 reshape.67
  72.4 5.8 %all-to-all-start.1 = ((f32[32,6,864]{2,1,0:T(8,128)}), f32[32,6,864]{2,1,0:T(8,128)S(1)}, u32[]{:S(2)}, u32[]{:S(2)}) async-start(f32[32,6,864]{2,1,0:T(8,128)} %reshape.67), calls=%async_computation.1 | async-start | bytes 1835008 | tf_op jit(solution)/shard_map/all_to_all | solution.py:87
  78.5 23.2 %all-to-all-done.1 = f32[32,6,864]{2,1,0:T(8,128)S(1)} async-done(((f32[32,6,864]{2,1,0:T(8,128)}), f32[32,6,864]{2,1,0:T(8,128)S(1)}, u32[]{:S(2)}, u32[]{:S(2)}) %all-to-all-start.1) | async-done | bytes 663584 | tf_op jit(solution)/shard_map/all_to_all | solution.py:87
  101.8 1.9 scatter_custom_fusion.2
  104.5 29.1 %all-gather.3.cloned.1.call-done = f32[768,864]{1,0:T(8,128)} async-done(((f32[96,864]{1,0:T(8,128)}), f32[768,864]{1,0:T(8,128)}) %all-gather.3.cloned.1.call-update) | async-done | bytes 2654224 | tf_op jit(solution)/shard_map/all_gather | solution.py:91
  133.6 3.0 %fusion.48 = (f32[768,288]{1,0:T(8,128)S(1)}, f32[768,288]{1,0:T(8,128)S(1)}, f32[768,288]{1,0:T(8,128)S(1)}) fusion(f32[768,864]{1,0:T(8,128)} %all-gather.3.cloned.1.call-done), kind=kLoop, calls=%fused_computation.85 | loop fusion | bytes 5308416 | tf_op jit(solution)/shard_map/slice | solution.py:49
  136.6 3.2 %fusion.49 = (f32[768,144]{1,0:T(8,128)}, f32[768,144]{1,0:T(8,128)}, f32[768,144]{1,0:T(8,128)}, f32[768,144]{1,0:T(8,128)}, f32[768,144]{1,0:T(8,128)}, /*index=5*/f32[768,144]{1,0:T(8,128)}) fusion(f32[768,864]{1,0:T(8,128)S(1)} %copy-done), kind=kLoop, calls=%fused_computation.86 | loop fusion | flops 331776 | bytes 5308416 | tf_op jit(solution)/shard_map/slice | solution.py:50
  139.8 29.2 %all-gather.5.cloned.1.call-done = f32[384,864]{1,0:T(8,128)} async-done(((f32[96,864]{1,0:T(8,128)}), f32[384,864]{1,0:T(8,128)}) %all-gather.5.cloned.1.call-update) | async-done | bytes 1327120 | tf_op jit(solution)/shard_map/all_gather | solution.py:92
  169.0 6.7 %fusion.1 = bf16[1536,384]{1,0:T(8,128)(2,1)S(1)} fusion(f32[768,144]{1,0:T(8,128)} %get-tuple-element.16, f32[768,144]{1,0:T(8,128)} %get-tuple-element.11, f32[768,288]{1,0:T(8,128)S(1)} %get-tuple-element.8, f32[384,864]{1,0:T(8,128)} %all-gather.5.cloned.1.call-done), kind=kOutput, calls=%fused_computation.13 | convolution fusion | flops 2040496128 | bytes 4227072 | tf_op jit(solution)/shard_map/dot_general | solution.py:53
  175.7 4.8 %fusion.2 = bf16[1536,384]{1,0:T(8,128)(2,1)S(1)} fusion(f32[768,144]{1,0:T(8,128)S(1)} %copy-done.3, f32[768,144]{1,0:T(8,128)S(1)} %copy-done.4, f32[768,288]{1,0:T(8,128)S(1)} %get-tuple-element.10, f32[384,864]{1,0:T(8,128)S(1)} %copy-done.5), kind=kOutput, calls=%fused_computation.14 | convolution fusion | flops 2040496128 | bytes 4521984 | tf_op jit(solution)/shard_map/dot_general | solution.py:53
  180.5 4.7 %fusion.3 = bf16[1536,384]{1,0:T(8,128)(2,1)S(1)} fusion(f32[768,144]{1,0:T(8,128)S(1)} %copy-done.1, f32[768,144]{1,0:T(8,128)S(1)} %copy-done.2, f32[768,288]{1,0:T(8,128)S(1)} %get-tuple-element.9, f32[384,864]{1,0:T(8,128)S(1)} %copy-done.5), kind=kOutput, calls=%fused_computation.15 | convolution fusion | flops 2040496128 | bytes 4521984 | tf_op jit(solution)/shard_map/dot_general | solution.py:53
  185.3 2.0 %pad_maximum_fusion = bf16[3,2,768,384]{3,2,1,0:T(8,128)(2,1)} fusion(bf16[1,2,768,384]{3,2,1,0:T(8,128)(2,1)S(1)} %bitcast.58, bf16[1,2,768,384]{3,2,1,0:T(8,128)(2,1)S(1)} %bitcast.57, bf16[1,2,768,384]{3,2,1,0:T(8,128)(2,1)S(1)} %bitcast.56), kind=kLoop, calls=%fused_computation.9 | loop fusion | flops 3538944 | bytes 7077888 | tf_op jit(solution)/shard_map/stack | solution.py:63
  (35 shorter events, 5.4 us)
Async XLA Ops:
  11.6 60.8 %all-to-all-start = ((s32[32,1,6]{2,1,0:T(1,128)}), s32[32,1,6]{2,1,0:T(1,128)S(1)}, u32[]{:S(2)}, u32[]{:S(2)}) async-start(s32[32,1,6]{2,1,0:T(1,128)} %bitcast.2), calls=%async_computation | async-start | bytes 32768 | tf_op jit(solution)/shard_map/all_to_all | solution.py:88
  72.4 29.3 %all-to-all-start.1 = ((f32[32,6,864]{2,1,0:T(8,128)}), f32[32,6,864]{2,1,0:T(8,128)S(1)}, u32[]{:S(2)}, u32[]{:S(2)}) async-start(f32[32,6,864]{2,1,0:T(8,128)} %reshape.67), calls=%async_computation.1 | async-start | bytes 1835008 | tf_op jit(solution)/shard_map/all_to_all | solution.py:87
  78.2 55.3 %all-gather.3.cloned.1.call-start = ((), (), s32[]{:S(2)}) async-start(), calls=%async_computation.2 | async-start | bytes 3096576 | tf_op jit(solution)/shard_map/all_gather | solution.py:91
  103.7 65.3 %all-gather.5.cloned.1.call-start = ((), (), s32[]{:S(2)}) async-start(), calls=%async_computation.3 | async-start | bytes 1720320 | tf_op jit(solution)/shard_map/all_gather | solution.py:92
  133.6 3.0 %copy-start = (f32[768,864]{1,0:T(8,128)S(1)}, f32[768,864]{1,0:T(8,128)}, u32[]{:S(2)}) copy-start(f32[768,864]{1,0:T(8,128)} %all-gather.3.cloned.1.call-done) | copy-start | bytes 7962628
  169.0 6.7 %copy-start.3 = (f32[768,144]{1,0:T(8,128)S(1)}, f32[768,144]{1,0:T(8,128)}, u32[]{:S(2)}) copy-start(f32[768,144]{1,0:T(8,128)} %get-tuple-element.14) | copy-start | bytes 1327108
  169.0 6.7 %copy-start.4 = (f32[768,144]{1,0:T(8,128)S(1)}, f32[768,144]{1,0:T(8,128)}, u32[]{:S(2)}) copy-start(f32[768,144]{1,0:T(8,128)} %get-tuple-element.15) | copy-start | bytes 1327108
  169.0 6.7 %copy-start.5 = (f32[384,864]{1,0:T(8,128)S(1)}, f32[384,864]{1,0:T(8,128)}, u32[]{:S(2)}) copy-start(f32[384,864]{1,0:T(8,128)} %all-gather.5.cloned.1.call-done) | copy-start | bytes 3981316
  175.7 4.8 %copy-start.1 = (f32[768,144]{1,0:T(8,128)S(1)}, f32[768,144]{1,0:T(8,128)}, u32[]{:S(2)}) copy-start(f32[768,144]{1,0:T(8,128)} %get-tuple-element.12) | copy-start | bytes 1327108
  175.7 4.8 %copy-start.2 = (f32[768,144]{1,0:T(8,128)S(1)}, f32[768,144]{1,0:T(8,128)}, u32[]{:S(2)}) copy-start(f32[768,144]{1,0:T(8,128)} %get-tuple-element.13) | copy-start | bytes 1327108
Sparse Core Ops, SparseCore 0:
  103.9 29.6 all-gather.2
  135.1 33.8 all-gather.4
where the time goes:
time: 195 us; the launch traced here: 194 us
  waiting for transfers between devices  82 us (42%)
  other arithmetic  44.6 us (23%)
  local copies, waits for them, and re-layouts  23.7 us (12%)
  matrix products  16.2 us (8%)
  between operations  14.3 us (7%)
  starting transfers between devices  13.4 us (7%)
    all_gather x1, waiting for transfers between devices, shards(): lax.all_gather(white, 'row', axis=0, tiled=True)  29.2 us
    all_gather x1, waiting for transfers between devices, shards(): row_stations = lax.all_gather(white, 'col', axis=0, tiled=True)  29.1 us
    all_to_all x1, waiting for transfers between devices, shards(): lax.all_to_all(packed, ('row', 'col'), split_axis=0, concat_axis=0, tiled...  23.2 us
    dot_general x3, matrix products, pair_tile(): lax.dot_general(stacked, other, (((1,), (1,)), ((), ())), precision=lax.P...  16.2 us
    unnamed x13, local copies, waits for them, and re-layouts  13.7 us
    convert_element_type x1, other arithmetic, whiten(): values = raw.astype(jnp.float32)  12.9 us
    add x1, other arithmetic, whiten(): energy = real_part * real_part + imag_part * imag_part  12 us
    all_to_all x1, starting transfers between devices, shards(): lax.all_to_all(labels, ('row', 'col'), split_axis=0, concat_axis=0, tiled...  7.3 us
  transfers between devices with their start and end apart: 4, of which 3 were waited for; matrix products, arithmetic and copies ran while one was open for 31% of the time, Pallas kernels for 0%

commit v1 on v0

v1 whole, which is shorter than its diff:
```python
import functools
import math

import jax
import jax.numpy as jnp
from jax import lax
from jax.experimental import pallas as pl
from jax.experimental.pallas import tpu as pltpu
from jax.sharding import PartitionSpec as P

power_floor = 0.25
bins = 3
lanes = 128
group = 8
slab = 8
full = 32767.0
vmem_bytes = 48 * 1024 * 1024

tail_tile = 2 * bins
width = (tail_tile + 1) * lanes


def meta_lane(segments):
    return tail_tile * (segments - lanes)


def dot_t(a, b):
    return lax.dot_general(a, b, (((1,), (1,)), ((), ())), preferred_element_type=jnp.float32)


def split(q):
    high = jnp.floor((q + 128.0) * (1.0 / 256.0))
    return (high * 256.0).astype(jnp.bfloat16), (q - high * 256.0).astype(jnp.bfloat16)


def iota(shape, dim):
    return lax.broadcasted_iota(jnp.int32, shape, dim)


def whiten_kernel(home_rows, count_ref, ids_ref, x_ref, out_ref, sel_ref, win_ref, id_ref, coded_ref):
    step = pl.program_id(0)
    slots_step, segments, two_band = x_ref.shape
    band = two_band // 2
    tail = segments - lanes
    slot_count = ids_ref.shape[1]
    rows = 2 * bins * group

    @pl.when(step == 0)
    def _():
        row = iota((rows, group * two_band), 0)
        col = iota((rows, group * two_band), 1)
        part = row // group
        same = (row % group) == (col // two_band)
        lane = col % two_band
        lower = (part // 2) * (band // 4)
        center = (part % 2) * band + lower + band // 4
        one = jnp.float32(1.0)
        sel_ref[...] = jnp.where(same & (lane == center), one, 0.0).astype(jnp.bfloat16)
        within = lane % band
        inside = (within >= lower) & (within < lower + band // 2)
        win_ref[...] = jnp.where(same & inside, one, 0.0).astype(jnp.bfloat16)
        ids = ids_ref[...].astype(jnp.float32)
        local = ids - home_rows * jnp.floor((ids + 0.5) * (1.0 / home_rows))
        eye = iota((slot_count, slot_count), 0) == iota((slot_count, slot_count), 1)
        id_ref[...] = jnp.sum(jnp.where(eye, local + 1.0, 0.0), axis=1, keepdims=True)

    def body(g, carry):
        x = x_ref[pl.ds(g * group, group)]
        xs = jnp.concatenate([x[s] for s in range(group)], axis=1)
        xf = xs.astype(jnp.float32)
        energy = xf * xf
        high = energy.astype(jnp.bfloat16)
        low = (energy - high.astype(jnp.float32)).astype(jnp.bfloat16)
        picked = dot_t(sel_ref[...], xs)
        total = dot_t(win_ref[...], high) + dot_t(win_ref[...], low)
        white = picked / jnp.sqrt(jnp.maximum(total * (2.0 / band), power_floor))
        first = pl.multiple_of(step * slots_step + g * group, group)
        coded = []
        expos = []
        mants = []
        for f in range(bins):
            pair = white[2 * f * group : 2 * (f + 1) * group]
            size = jnp.maximum(jnp.abs(pair[:group]), jnp.abs(pair[group:]))
            peak = jnp.maximum(jnp.max(size, axis=1, keepdims=True), 1e-30)
            expo = jnp.ceil(jnp.log2(peak))
            mant = jnp.floor(peak * jnp.exp2(-expo) * 16384.0) + 1.0
            inverse = (full * 16384.0) / (mant * jnp.exp2(expo))
            expos.append(expo)
            mants.append(mant)
            for p in range(2):
                q = jnp.round(pair[p * group : (p + 1) * group] * inverse)
                coded.append(jnp.clip(q, -full, full))
        for t in range(tail_tile):
            coded_ref[pl.ds(first, group), t * lanes : (t + 1) * lanes] = coded[t][:, :lanes]
        last = [c[:, lanes:] for c in coded] + mants + expos + [id_ref[pl.ds(first, group), :]]
        used = tail_tile * tail + 2 * bins + 1
        last.append(jnp.zeros((group, lanes - used), jnp.float32))
        coded_ref[pl.ds(first, group), tail_tile * lanes :] = jnp.concatenate(last, axis=1)
        return carry

    lax.fori_loop(0, slots_step // group, body, 0)

    @pl.when(step == pl.num_programs(0) - 1)
    def _():
        ids = ids_ref[...].astype(jnp.float32)
        target = jnp.floor((ids + 0.5) * (1.0 / home_rows))
        shape = (slot_count, slot_count)
        j = iota(shape, 0)
        i = iota(shape, 1)
        target_column = jnp.sum(jnp.where(j == i, target, 0.0), axis=1, keepdims=True)
        count = count_ref[0]
        ahead = (j < i) & (j < count) & (target_column == target)
        within = jnp.sum(jnp.where(ahead, 1.0, 0.0), axis=0, keepdims=True)
        live = iota((1, slot_count), 1) < count
        place = jnp.where(live, target * slab + within, -1.0)
        send_rows = out_ref.shape[0]
        spot = iota((send_rows, slot_count), 0).astype(jnp.float32)
        chosen = jnp.where(spot == place, 1.0, 0.0).astype(jnp.bfloat16)
        high, low = split(coded_ref[...])
        sent = jnp.dot(chosen, high, preferred_element_type=jnp.float32)
        sent += jnp.dot(chosen, low, preferred_element_type=jnp.float32)
        out_ref[...] = sent.astype(jnp.int32).astype(jnp.int16)


def whiten_pack(spectra, station_ids, counts, readers):
    slot_count, segments, two_band = spectra.shape
    home_rows = slot_count // 2
    slots_step = 32
    rows = 2 * bins * group
    return pl.pallas_call(
        functools.partial(whiten_kernel, home_rows),
        grid=(slot_count // slots_step,),
        out_shape=jax.ShapeDtypeStruct((readers * slab, width), jnp.int16),
        in_specs=[
            pl.BlockSpec(memory_space=pltpu.SMEM),
            pl.BlockSpec((1, slot_count), lambda i: (0, 0)),
            pl.BlockSpec((slots_step, segments, two_band), lambda i: (i, 0, 0)),
        ],
        out_specs=pl.BlockSpec((readers * slab, width), lambda i: (0, 0)),
        scratch_shapes=[
            pltpu.VMEM((rows, group * two_band), jnp.bfloat16),
            pltpu.VMEM((rows, group * two_band), jnp.bfloat16),
            pltpu.VMEM((slot_count, 1), jnp.float32),
            pltpu.VMEM((slot_count, width), jnp.float32),
        ],
        compiler_params=pltpu.CompilerParams(vmem_limit_bytes=vmem_bytes),
        name="whiten_pack",
    )(counts, station_ids.reshape(1, slot_count), spectra)


def settle_kernel(id_lane, in_ref, out_ref):
    home_rows = out_ref.shape[0]
    q = in_ref[...].astype(jnp.int32).astype(jnp.float32)
    station = q[:, id_lane : id_lane + 1]
    wanted = (iota((q.shape[0], home_rows), 1) + 1).astype(jnp.float32)
    chosen = jnp.where(station == wanted, 1.0, 0.0).astype(jnp.bfloat16)
    high, low = split(q)
    dims = (((0,), (0,)), ((), ()))
    home = lax.dot_general(chosen, high, dims, preferred_element_type=jnp.float32)
    home += lax.dot_general(chosen, low, dims, preferred_element_type=jnp.float32)
    out_ref[...] = home.astype(jnp.int32).astype(jnp.int16)


def settle(received, home_rows, segments):
    id_lane = tail_tile * lanes + meta_lane(segments) + 2 * bins
    return pl.pallas_call(
        functools.partial(settle_kernel, id_lane),
        out_shape=jax.ShapeDtypeStruct((home_rows, width), jnp.int16),
        compiler_params=pltpu.CompilerParams(vmem_limit_bytes=vmem_bytes),
        name="settle",
    )(received)


def roll(x, shift):
    return pltpu.roll(x, shift % x.shape[1], 1)


def pair_kernel(segments, row_n, col_n, place_ref, *refs):
    row_refs = refs[:row_n]
    col_refs = refs[row_n : row_n + col_n]
    out_ref, a_ref, b_ref, scale_ref, tail_ref = refs[row_n + col_n :]
    f = pl.program_id(0)
    home_rows = row_refs[0].shape[0]
    tail = segments - lanes
    meta = meta_lane(segments)
    columns = col_n * home_rows
    lane = iota((home_rows, lanes), 1)
    unit = 1.0 / (16384.0 * full)

    def load(ref):
        start = pl.multiple_of(f * 2 * lanes, 2 * lanes)
        main = ref[:, pl.ds(start, 2 * lanes)].astype(jnp.int32).astype(jnp.float32)
        last = ref[:, tail_tile * lanes :].astype(jnp.int32).astype(jnp.float32)
        mine = pltpu.roll(last, lax.rem(lanes - f * 2 * tail, lanes), 1)
        return main, last, jnp.where(lane < 2 * tail, mine, 0.0)

    def ends(first, second, third):
        return first + roll(second, 2 * tail) + roll(third, 4 * tail)

    def wide(x):
        return x[0].astype(jnp.float32), x[1].astype(jnp.float32)

    for k in range(row_n):
        main, last, mine = load(row_refs[k])
        start = pl.multiple_of(place_ref[0, k] * home_rows, home_rows)
        high, low = split(main)
        tail_high, tail_low = wide(split(mine))
        ending = ends(tail_high, tail_low, tail_high).astype(jnp.bfloat16)
        a_ref[pl.ds(start, home_rows), :] = jnp.concatenate([high, low, high, ending], axis=1)
        power = last * jnp.exp2(roll(last, -bins))
        scale = jnp.sum(jnp.where(lane == meta + f, power, 0.0), axis=1, keepdims=True)
        scale_ref[pl.ds(start, home_rows), :] = scale * unit

    for k in range(col_n):
        main, last, mine = load(col_refs[k])
        turned = jnp.concatenate([-main[:, lanes:], main[:, :lanes]], axis=1)
        mine_turned = jnp.where(lane < tail, -roll(mine, -tail), roll(mine, tail))
        mine_turned = jnp.where(lane < 2 * tail, mine_turned, 0.0)
        start = pl.multiple_of(place_ref[1, k] * home_rows, home_rows)
        for offset, value, end in ((0, main, mine), (columns, turned, mine_turned)):
            high, low = split(value)
            tail_high, tail_low = wide(split(end))
            ending = ends(tail_high, tail_high, tail_low).astype(jnp.bfloat16)
            b_ref[pl.ds(offset + start, home_rows), :] = jnp.concatenate([high, high, low, ending], axis=1)
        tail_ref[pl.ds(start, home_rows), :] = last

    pick = iota((8, lanes), 0)
    want = jnp.where(pick == 0, meta + f, meta + bins + f)
    chosen = jnp.where((iota((8, lanes), 1) == want) & (pick < 2), 1.0, 0.0).astype(jnp.bfloat16)
    high, low = split(tail_ref[...])
    codes = dot_t(chosen, high) + dot_t(chosen, low)
    column_scale = codes[0:1] * jnp.exp2(codes[1:2]) * (unit / math.sqrt(segments))

    product = dot_t(a_ref[...], b_ref[...])
    row_scale = scale_ref[...]
    for p in range(2):
        value = product[:, p * columns : (p + 1) * columns] * row_scale * column_scale
        out_ref[0, p] = value.astype(jnp.bfloat16)


def pair_tiles(row_blocks, row_index, col_blocks, col_index, segments):
    row_n, col_n = len(row_blocks), len(col_blocks)
    home_rows = row_blocks[0].shape[0]
    rows, columns = row_n * home_rows, col_n * home_rows
    most = max(row_n, col_n)
    place = jnp.stack([
        jnp.pad(row_index, (0, most - row_n)),
        jnp.pad(col_index, (0, most - col_n)),
    ])
    block = pl.BlockSpec((home_rows, width), lambda f, place: (0, 0))
    depth = 7 * lanes
    return pl.pallas_call(
        functools.partial(pair_kernel, segments, row_n, col_n),
        grid_spec=pltpu.PrefetchScalarGridSpec(
            num_scalar_prefetch=1,
            grid=(bins,),
            in_specs=[block] * (row_n + col_n),
            out_specs=pl.BlockSpec((1, 2, rows, columns), lambda f, place: (f, 0, 0, 0)),
            scratch_shapes=[
                pltpu.VMEM((rows, depth), jnp.bfloat16),
                pltpu.VMEM((2 * columns, depth), jnp.bfloat16),
                pltpu.VMEM((rows, 1), jnp.float32),
                pltpu.VMEM((columns, lanes), jnp.float32),
            ],
        ),
        out_shape=jax.ShapeDtypeStruct((bins, 2, rows, columns), jnp.bfloat16),
        compiler_params=pltpu.CompilerParams(vmem_limit_bytes=vmem_bytes),
        name="pair_tiles",
    )(place, *row_blocks, *col_blocks)


def across(value, axis, distance):
    size = lax.axis_size(axis)
    return lax.ppermute(value, axis, [(i, i ^ distance) for i in range(size)])


def shards(spectra, station_ids, counts):
    row_count = lax.axis_size("row")
    column_count = lax.axis_size("col")
    readers = row_count * column_count
    slot_count, segments, _ = spectra.shape
    home_rows = slot_count // 2
    packed = whiten_pack(spectra, station_ids, counts, readers)
    received = lax.all_to_all(packed, ("row", "col"), split_axis=0, concat_axis=0, tiled=True)
    white = settle(received, home_rows, segments)
    row_blocks = [None] * column_count
    row_blocks[0] = white
    col_blocks = [white]
    for k in range(1, row_count):
        col_blocks.append(across(white, "row", k))
    for k in range(2, column_count, 2):
        row_blocks[k] = across(white, "col", k)
    for k in range(0, column_count, 2):
        row_blocks[k + 1] = across(row_blocks[k], "col", 1)
    row_index = lax.axis_index("col") ^ jnp.arange(column_count, dtype=jnp.int32)
    col_index = lax.axis_index("row") ^ jnp.arange(row_count, dtype=jnp.int32)
    return pair_tiles(row_blocks, row_index, col_blocks, col_index, segments)


def solution(mesh):
    in_specs = (P(("row", "col"), None, None), P(("row", "col")), P(("row", "col")))
    out_specs = P(None, None, "row", "col")
    return jax.shard_map(shards, mesh=mesh, in_specs=in_specs, out_specs=out_specs, check_vma=False)
```

time: 195 us -> 70.3 us (0.36)
  waiting for transfers between devices: 82 us -> 20.5 us
  other arithmetic: 44.6 us -> 0.02 us
  Pallas kernels: 0 us -> 26.9 us
  local copies, waits for them, and re-layouts: 23.7 us -> 0.68 us
  matrix products: 16.2 us -> 0 us
  between operations: 14.3 us -> 0.7 us
  starting transfers between devices: 13.4 us -> 21.2 us
    all_gather x2 -> x0, waiting for transfers between devices: 58.3 us -> none  [the longest x1 29.2 us: shards(): lax.all_gather(white, 'row', axis=0, tiled=True)]
    pallas_call x0 -> x3, Pallas kernels: none -> 26.9 us  [the longest x1 17.6 us: whiten_pack(): pl.pallas_call(functools.partial(whiten_kernel, home_rows), grid=(slot_co...]
    dot_general x3 -> x0, matrix products: 16.2 us -> none  [pair_tile(): lax.dot_general(stacked, other, (((1,), (1,)), ((), ())), precision=lax.P...]
    ppermute x0 -> x10, starting transfers between devices: none -> 13.9 us  [across(): return lax.ppermute(value, axis, [(i, i ^ distance) for i in range(size)])]
    unnamed x13 -> x2, local copies, waits for them, and re-layouts: 13.7 us -> 0.67 us
    convert_element_type x1 -> x0, other arithmetic: 12.9 us -> none  [whiten(): values = raw.astype(jnp.float32)]
    add x1 -> x0, other arithmetic: 12 us -> none  [whiten(): energy = real_part * real_part + imag_part * imag_part]
    all_to_all x1, waiting for transfers between devices: 23.2 us -> 14.4 us  [shards(): lax.all_to_all(packed, ('row', 'col'), split_axis=0, concat_axis=0, tiled...]
  transfers between devices with their start and end apart: 4 -> 11, of which waited for: 3 -> 4; matrix products, arithmetic and copies ran while one was open for 31% -> 0% of each run, Pallas kernels for 0% -> 0%
where the time goes in v1:
time: 70.3 us; the launch traced here: 70 us
  Pallas kernels  26.9 us (38%)
  starting transfers between devices  21.2 us (30%)
  waiting for transfers between devices  20.5 us (29%)
    pallas_call x1, Pallas kernels, whiten_pack(): pl.pallas_call(functools.partial(whiten_kernel, home_rows), grid=(slot_co...  17.6 us
    all_to_all x1, waiting for transfers between devices, shards(): lax.all_to_all(packed, ('row', 'col'), split_axis=0, concat_axis=0, tiled...  14.4 us
    ppermute x10, starting transfers between devices, across(): return lax.ppermute(value, axis, [(i, i ^ distance) for i in range(size)])  13.9 us
    pallas_call x1, Pallas kernels, pair_tiles(): pl.pallas_call(functools.partial(pair_kernel, segments, row_n, col_n), gr...  8.78 us
    all_to_all x1, starting transfers between devices, shards(): lax.all_to_all(packed, ('row', 'col'), split_axis=0, concat_axis=0, tiled...  7.3 us
    ppermute x10, waiting for transfers between devices, across(): return lax.ppermute(value, axis, [(i, i ^ distance) for i in range(size)])  6.15 us
  transfers between devices with their start and end apart: 11, of which 4 were waited for; matrix products, arithmetic and copies ran while one was open for 0% of the time, Pallas kernels for 0%

profile of v1, /device:TPU:0, one launch (start us, length us, event | category | flops | bytes accessed | tf_op | source)
XLA Modules:
  0.0 70.0 jit_solution(11638654131337700445)
XLA Ops:
  0.7 0.7 copy-done
  1.3 17.6 %whiten_pack.1 = s16[256,896]{1,0:T(8,128)(2,1)} custom-call(s32[1]{0:T(128)S(6)} %copy.4.count_ref, s32[1,192]{1,0:T(1,128)S(1)} %bitcast.6, bf16[192,144,128]{2,1,0:T(8,128)(2,1)} %x_ref.1), custom_call_target="tpu_custom_call" | custom-call | tf_op jit(solution)/shard_map/whiten_pack/pallas_call | solution.py:130
  19.0 7.3 %all-to-all-start = ((s16[32,8,896]{2,1,0:T(8,128)(2,1)}), s16[32,8,896]{2,1,0:T(8,128)(2,1)S(1)}, u32[]{:S(2)}, u32[]{:S(2)}) async-start(s16[32,8,896]{2,1,0:T(8,128)(2,1)} %bitcast.2), calls=%async_computation | async-start | bytes 917504 | tf_op jit(solution)/shard_map/all_to_all | solution.py:284
  26.3 14.4 %all-to-all-done = s16[32,8,896]{2,1,0:T(8,128)(2,1)S(1)} async-done(((s16[32,8,896]{2,1,0:T(8,128)(2,1)}), s16[32,8,896]{2,1,0:T(8,128)(2,1)S(1)}, u32[]{:S(2)}, u32[]{:S(2)}) %all-to-all-start) | async-done | bytes 458784 | tf_op jit(solution)/shard_map/all_to_all | solution.py:284
  40.6 0.5 settle.1.refs_0_.refs_8_
  41.1 1.2 %collective-permute-start.9 = (s16[96,896]{1,0:T(8,128)(2,1)S(1)}, s16[96,896]{1,0:T(8,128)(2,1)S(1)}, u32[]{:S(2)}, u32[]{:S(2)}) collective-permute-start(s16[96,896]{1,0:T(8,128)(2,1)S(1)} %settle.1.refs_0_.refs_8_), channel_id=1, source_target_pairs={{0,24},{8,16},{16,8},{24,0},{1,25},{9,17},{17,9},{25,1},{2,26},{10... | collective-permute-start | bytes 516104 | tf_op jit(solution)/shard_map/ppermute | solution.py:274
  42.3 1.5 %collective-permute-start.8 = (s16[96,896]{1,0:T(8,128)(2,1)S(1)}, s16[96,896]{1,0:T(8,128)(2,1)S(1)}, u32[]{:S(2)}, u32[]{:S(2)}) collective-permute-start(s16[96,896]{1,0:T(8,128)(2,1)S(1)} %settle.1.refs_0_.refs_8_), channel_id=1, source_target_pairs={{0,16},{8,24},{16,0},{24,8},{1,17},{9,25},{17,1},{25,9},{2,18},{10... | collective-permute-start | bytes 516104 | tf_op jit(solution)/shard_map/ppermute | solution.py:274
  43.8 0.7 %collective-permute-start.5 = (s16[96,896]{1,0:T(8,128)(2,1)S(1)}, s16[96,896]{1,0:T(8,128)(2,1)S(1)}, u32[]{:S(2)}, u32[]{:S(2)}) collective-permute-start(s16[96,896]{1,0:T(8,128)(2,1)S(1)} %settle.1.refs_0_.refs_8_), channel_id=1, source_target_pairs={{0,6},{1,7},{2,4},{3,5},{4,2},{5,3},{6,0},{7,1},{8,14},{9,15},{10,... | collective-permute-start | bytes 516104 | tf_op jit(solution)/shard_map/ppermute | solution.py:274
  44.5 1.0 %collective-permute-start.3 = (s16[96,896]{1,0:T(8,128)(2,1)S(1)}, s16[96,896]{1,0:T(8,128)(2,1)S(1)}, u32[]{:S(2)}, u32[]{:S(2)}) collective-permute-start(s16[96,896]{1,0:T(8,128)(2,1)S(1)} %settle.1.refs_0_.refs_8_), channel_id=1, source_target_pairs={{0,4},{1,5},{2,6},{3,7},{4,0},{5,1},{6,2},{7,3},{8,12},{9,13},{10,... | collective-permute-start | bytes 516104 | tf_op jit(solution)/shard_map/ppermute | solution.py:274
  45.5 1.8 %collective-permute-start.1 = (s16[96,896]{1,0:T(8,128)(2,1)S(1)}, s16[96,896]{1,0:T(8,128)(2,1)S(1)}, u32[]{:S(2)}, u32[]{:S(2)}) collective-permute-start(s16[96,896]{1,0:T(8,128)(2,1)S(1)} %settle.1.refs_0_.refs_8_), channel_id=1, source_target_pairs={{0,2},{1,3},{2,0},{3,1},{4,6},{5,7},{6,4},{7,5},{8,10},{9,11},{10,... | collective-permute-start | bytes 516104 | tf_op jit(solution)/shard_map/ppermute | solution.py:274
  47.3 3.0 %collective-permute-done.9.refs_11_ = s16[96,896]{1,0:T(8,128)(2,1)S(1)} collective-permute-done((s16[96,896]{1,0:T(8,128)(2,1)S(1)}, s16[96,896]{1,0:T(8,128)(2,1)S(1)}, u32[]{:S(2)}, u32[]{:S(2)}) %collective-permute-start.9) | collective-permute-done | bytes 172064 | tf_op jit(solution)/shard_map/ppermute | solution.py:274
  50.3 6.7 %collective-permute-start.7 = (s16[96,896]{1,0:T(8,128)(2,1)S(1)}, s16[96,896]{1,0:T(8,128)(2,1)S(1)}, u32[]{:S(2)}, u32[]{:S(2)}) collective-permute-start(s16[96,896]{1,0:T(8,128)(2,1)S(1)} %settle.1.refs_0_.refs_8_), channel_id=1, source_target_pairs={{0,8},{8,0},{16,24},{24,16},{1,9},{9,1},{17,25},{25,17},{2,10},{10... | collective-permute-start | bytes 516104 | tf_op jit(solution)/shard_map/ppermute | solution.py:274
  57.0 1.4 %collective-permute-done.8.refs_10_ = s16[96,896]{1,0:T(8,128)(2,1)S(1)} collective-permute-done((s16[96,896]{1,0:T(8,128)(2,1)S(1)}, s16[96,896]{1,0:T(8,128)(2,1)S(1)}, u32[]{:S(2)}, u32[]{:S(2)}) %collective-permute-start.8) | collective-permute-done | bytes 172064 | tf_op jit(solution)/shard_map/ppermute | solution.py:274
  58.4 0.0 collective-permute-start
  58.4 0.0 collective-permute-done.5.refs_6_
  58.5 0.5 collective-permute-start.6
  59.0 0.1 collective-permute-start.4
  59.0 0.4 collective-permute-start.2
  59.5 1.7 %collective-permute-done.7.refs_9_ = s16[96,896]{1,0:T(8,128)(2,1)S(1)} collective-permute-done((s16[96,896]{1,0:T(8,128)(2,1)S(1)}, s16[96,896]{1,0:T(8,128)(2,1)S(1)}, u32[]{:S(2)}, u32[]{:S(2)}) %collective-permute-start.7) | collective-permute-done | bytes 172064 | tf_op jit(solution)/shard_map/ppermute | solution.py:274
  61.2 0.0 collective-permute-done.refs_1_
  61.2 0.0 collective-permute-done.6.refs_7_
  61.2 0.0 collective-permute-done.4.refs_5_
  61.2 0.0 collective-permute-done.2.refs_3_
  61.2 8.8 %pair_tiles.1 = bf16[3,2,768,384]{3,2,1,0:T(8,128)(2,1)} custom-call(s32[2,8]{1,0:T(2,128)S(1)} %pad_add_fusion.place_ref, s16[96,896]{1,0:T(8,128)(2,1)S(1)} %settle.1.refs_0_.refs_8_, s16[96,896]{1,0:T(8,128)(2,1)S(1)} %collective-permute-done.refs_1_, s16[96,896]{1,0:T(8,128)(2,1)S(1)} %collective-permute-done.1.refs_2_, ...), custom_call_target="tpu_custom_call" | custom-call | tf_op jit(solution)/shard_map/pair_tiles/pallas_call | solution.py:252
  (7 shorter events, 0.0 us)
Async XLA Ops:
  0.7 0.7 copy-start
  19.0 21.7 %all-to-all-start = ((s16[32,8,896]{2,1,0:T(8,128)(2,1)}), s16[32,8,896]{2,1,0:T(8,128)(2,1)S(1)}, u32[]{:S(2)}, u32[]{:S(2)}) async-start(s16[32,8,896]{2,1,0:T(8,128)(2,1)} %bitcast.2), calls=%async_computation | async-start | bytes 917504 | tf_op jit(solution)/shard_map/all_to_all | solution.py:284
  41.1 9.2 %collective-permute-start.9 = (s16[96,896]{1,0:T(8,128)(2,1)S(1)}, s16[96,896]{1,0:T(8,128)(2,1)S(1)}, u32[]{:S(2)}, u32[]{:S(2)}) collective-permute-start(s16[96,896]{1,0:T(8,128)(2,1)S(1)} %settle.1.refs_0_.refs_8_), channel_id=1, source_target_pairs={{0,24},{8,16},{16,8},{24,0},{1,25},{9,17},{17,9},{25,1},{2,26},{10... | collective-permute-start | bytes 516104 | tf_op jit(solution)/shard_map/ppermute | solution.py:274
  42.3 16.2 %collective-permute-start.8 = (s16[96,896]{1,0:T(8,128)(2,1)S(1)}, s16[96,896]{1,0:T(8,128)(2,1)S(1)}, u32[]{:S(2)}, u32[]{:S(2)}) collective-permute-start(s16[96,896]{1,0:T(8,128)(2,1)S(1)} %settle.1.refs_0_.refs_8_), channel_id=1, source_target_pairs={{0,16},{8,24},{16,0},{24,8},{1,17},{9,25},{17,1},{25,9},{2,18},{10... | collective-permute-start | bytes 516104 | tf_op jit(solution)/shard_map/ppermute | solution.py:274
  43.8 14.6 %collective-permute-start.5 = (s16[96,896]{1,0:T(8,128)(2,1)S(1)}, s16[96,896]{1,0:T(8,128)(2,1)S(1)}, u32[]{:S(2)}, u32[]{:S(2)}) collective-permute-start(s16[96,896]{1,0:T(8,128)(2,1)S(1)} %settle.1.refs_0_.refs_8_), channel_id=1, source_target_pairs={{0,6},{1,7},{2,4},{3,5},{4,2},{5,3},{6,0},{7,1},{8,14},{9,15},{10,... | collective-permute-start | bytes 516104 | tf_op jit(solution)/shard_map/ppermute | solution.py:274
  44.5 14.4 %collective-permute-start.3 = (s16[96,896]{1,0:T(8,128)(2,1)S(1)}, s16[96,896]{1,0:T(8,128)(2,1)S(1)}, u32[]{:S(2)}, u32[]{:S(2)}) collective-permute-start(s16[96,896]{1,0:T(8,128)(2,1)S(1)} %settle.1.refs_0_.refs_8_), channel_id=1, source_target_pairs={{0,4},{1,5},{2,6},{3,7},{4,0},{5,1},{6,2},{7,3},{8,12},{9,13},{10,... | collective-permute-start | bytes 516104 | tf_op jit(solution)/shard_map/ppermute | solution.py:274
  45.5 13.5 %collective-permute-start.1 = (s16[96,896]{1,0:T(8,128)(2,1)S(1)}, s16[96,896]{1,0:T(8,128)(2,1)S(1)}, u32[]{:S(2)}, u32[]{:S(2)}) collective-permute-start(s16[96,896]{1,0:T(8,128)(2,1)S(1)} %settle.1.refs_0_.refs_8_), channel_id=1, source_target_pairs={{0,2},{1,3},{2,0},{3,1},{4,6},{5,7},{6,4},{7,5},{8,10},{9,11},{10,... | collective-permute-start | bytes 516104 | tf_op jit(solution)/shard_map/ppermute | solution.py:274
  50.3 10.9 %collective-permute-start.7 = (s16[96,896]{1,0:T(8,128)(2,1)S(1)}, s16[96,896]{1,0:T(8,128)(2,1)S(1)}, u32[]{:S(2)}, u32[]{:S(2)}) collective-permute-start(s16[96,896]{1,0:T(8,128)(2,1)S(1)} %settle.1.refs_0_.refs_8_), channel_id=1, source_target_pairs={{0,8},{8,0},{16,24},{24,16},{1,9},{9,1},{17,25},{25,17},{2,10},{10... | collective-permute-start | bytes 516104 | tf_op jit(solution)/shard_map/ppermute | solution.py:274
  58.4 2.8 %collective-permute-start = (s16[96,896]{1,0:T(8,128)(2,1)S(1)}, s16[96,896]{1,0:T(8,128)(2,1)S(1)}, u32[]{:S(2)}, u32[]{:S(2)}) collective-permute-start(s16[96,896]{1,0:T(8,128)(2,1)S(1)} %settle.1.refs_0_.refs_8_), channel_id=1, source_target_pairs={{0,1},{1,0},{2,3},{3,2},{4,5},{5,4},{6,7},{7,6},{8,9},{9,8},{10,11... | collective-permute-start | bytes 516104 | tf_op jit(solution)/shard_map/ppermute | solution.py:274
  58.5 2.8 %collective-permute-start.6 = (s16[96,896]{1,0:T(8,128)(2,1)S(1)}, s16[96,896]{1,0:T(8,128)(2,1)S(1)}, u32[]{:S(2)}, u32[]{:S(2)}) collective-permute-start(s16[96,896]{1,0:T(8,128)(2,1)S(1)} %collective-permute-done.5.refs_6_), channel_id=1, source_target_pairs={{0,1},{1,0},{2,3},{3,2},{4,5},{5,4},{6,7},{7,6},{8,9},{9,8},{10,11... | collective-permute-start | bytes 516104 | tf_op jit(solution)/shard_map/ppermute | solution.py:274
  59.0 2.3 %collective-permute-start.4 = (s16[96,896]{1,0:T(8,128)(2,1)S(1)}, s16[96,896]{1,0:T(8,128)(2,1)S(1)}, u32[]{:S(2)}, u32[]{:S(2)}) collective-permute-start(s16[96,896]{1,0:T(8,128)(2,1)S(1)} %collective-permute-done.3.refs_4_), channel_id=1, source_target_pairs={{0,1},{1,0},{2,3},{3,2},{4,5},{5,4},{6,7},{7,6},{8,9},{9,8},{10,11... | collective-permute-start | bytes 516104 | tf_op jit(solution)/shard_map/ppermute | solution.py:274
  59.0 2.2 %collective-permute-start.2 = (s16[96,896]{1,0:T(8,128)(2,1)S(1)}, s16[96,896]{1,0:T(8,128)(2,1)S(1)}, u32[]{:S(2)}, u32[]{:S(2)}) collective-permute-start(s16[96,896]{1,0:T(8,128)(2,1)S(1)} %collective-permute-done.1.refs_2_), channel_id=1, source_target_pairs={{0,1},{1,0},{2,3},{3,2},{4,5},{5,4},{6,7},{7,6},{8,9},{9,8},{10,11... | collective-permute-start | bytes 516104 | tf_op jit(solution)/shard_map/ppermute | solution.py:274

commit v2 on v1

--- a/solution.py
+++ b/solution.py
@@ -29,58 +29,99 @@
 
 
 def split(q):
-    high = jnp.floor((q + 128.0) * (1.0 / 256.0))
-    return (high * 256.0).astype(jnp.bfloat16), (q - high * 256.0).astype(jnp.bfloat16)
+    high = q.astype(jnp.bfloat16)
+    return high, (q - high.astype(jnp.float32)).astype(jnp.bfloat16)
 
 
 def iota(shape, dim):
     return lax.broadcasted_iota(jnp.int32, shape, dim)
 
 
-def whiten_kernel(home_rows, count_ref, ids_ref, x_ref, out_ref, sel_ref, win_ref, id_ref, coded_ref):
-    step = pl.program_id(0)
-    slots_step, segments, two_band = x_ref.shape
+def roll(x, shift):
+    return pltpu.roll(x, shift % x.shape[1], 1)
+
+
+def whiten_kernel(home_rows, parts, count_ref, ids_ref, source_ref, out_ref, x_ref, weight_ref, id_ref, coded_ref, found_ref, sems):
+    slot_count, segments, two_band = x_ref.shape
+    edges = [slot_count * e // parts[-1] for e in parts]
+    copies = []
+    for c in range(len(parts) - 1):
+        span = pl.ds(edges[c], edges[c + 1] - edges[c])
+        copies.append(pltpu.make_async_copy(source_ref.at[span], x_ref.at[span], sems.at[c]))
+        copies[c].start()
     band = two_band // 2
     tail = segments - lanes
-    slot_count = ids_ref.shape[1]
-    rows = 2 * bins * group
-
-    @pl.when(step == 0)
-    def _():
-        row = iota((rows, group * two_band), 0)
-        col = iota((rows, group * two_band), 1)
-        part = row // group
-        same = (row % group) == (col // two_band)
-        lane = col % two_band
-        lower = (part // 2) * (band // 4)
-        center = (part % 2) * band + lower + band // 4
-        one = jnp.float32(1.0)
-        sel_ref[...] = jnp.where(same & (lane == center), one, 0.0).astype(jnp.bfloat16)
-        within = lane % band
-        inside = (within >= lower) & (within < lower + band // 2)
-        win_ref[...] = jnp.where(same & inside, one, 0.0).astype(jnp.bfloat16)
-        ids = ids_ref[...].astype(jnp.float32)
-        local = ids - home_rows * jnp.floor((ids + 0.5) * (1.0 / home_rows))
-        eye = iota((slot_count, slot_count), 0) == iota((slot_count, slot_count), 1)
-        id_ref[...] = jnp.sum(jnp.where(eye, local + 1.0, 0.0), axis=1, keepdims=True)
-
-    def body(g, carry):
-        x = x_ref[pl.ds(g * group, group)]
-        xs = jnp.concatenate([x[s] for s in range(group)], axis=1)
-        xf = xs.astype(jnp.float32)
-        energy = xf * xf
-        high = energy.astype(jnp.bfloat16)
-        low = (energy - high.astype(jnp.float32)).astype(jnp.bfloat16)
-        picked = dot_t(sel_ref[...], xs)
-        total = dot_t(win_ref[...], high) + dot_t(win_ref[...], low)
-        white = picked / jnp.sqrt(jnp.maximum(total * (2.0 / band), power_floor))
-        first = pl.multiple_of(step * slots_step + g * group, group)
-        coded = []
+    depth = group * two_band
+
+    row = iota((lanes, depth), 0)
+    col = iota((lanes, depth), 1)
+    part = row // group
+    same = (row % group) == (col // two_band)
+    lane = col % two_band
+    lower = (part // 2) * (band // 4)
+    center = (part % 2) * band + lower + band // 4
+    picks = same & (part < 2 * bins) & (lane == center)
+    weight_ref[:, :depth] = jnp.where(picks, 1.0, 0.0).astype(jnp.bfloat16)
+    half = depth // 2
+    row = iota((lanes, half), 0)
+    col = iota((lanes, half), 1)
+    part = row // group
+    lower = (part - 2 * bins) * (band // 4)
+    within = col % band
+    inside = (row % group == col // band) & (part >= 2 * bins) & (part < 3 * bins)
+    inside = inside & (within >= lower) & (within < lower + band // 2)
+    window = jnp.where(inside, 1.0, 0.0).astype(jnp.bfloat16)
+    weight_ref[:, depth : depth + half] = window
+    weight_ref[:, depth + half :] = window
+    left = iota((segments, two_band), 1) < band
+    ids = ids_ref[...].astype(jnp.float32)
+    local = ids - home_rows * jnp.floor((ids + 0.5) * (1.0 / home_rows))
+    eye = iota((slot_count, slot_count), 0) == iota((slot_count, slot_count), 1)
+    id_ref[...] = jnp.sum(jnp.where(eye, local + 1.0, 0.0), axis=1, keepdims=True)
+
+    target = jnp.floor((ids + 0.5) * (1.0 / home_rows))
+    shape = (slot_count, slot_count)
+    j = iota(shape, 0)
+    i = iota(shape, 1)
+    target_column = jnp.sum(jnp.where(j == i, target, 0.0), axis=1, keepdims=True)
+    count = count_ref[0]
+    ahead = (j < i) & (j < count) & (target_column == target)
+    within = jnp.sum(jnp.where(ahead, 1.0, 0.0), axis=0, keepdims=True)
+    live = iota((1, slot_count), 1) < count
+    place = jnp.where(live, target * slab + within, -1.0)
+    send_rows = out_ref.shape[0]
+    spot = iota((send_rows, slot_count), 0).astype(jnp.float32)
+    chosen = jnp.where(spot == place, 1.0, 0.0).astype(jnp.bfloat16)
+
+    for c in range(len(parts) - 1):
+        copies[c].wait()
+        for start in range(edges[c], edges[c + 1], group):
+            x = x_ref[start : start + group]
+            xs = jnp.concatenate([x[s] for s in range(group)], axis=1)
+            folded = []
+            for s in range(0, group, 2):
+                pair = []
+                for xf in (x[s].astype(jnp.float32), x[s + 1].astype(jnp.float32)):
+                    energy = xf * xf
+                    pair.append(energy + roll(energy, band))
+                folded.append(jnp.where(left, pair[0], pair[1]))
+            folded = jnp.concatenate(folded, axis=1)
+            high = folded.astype(jnp.bfloat16)
+            low = (folded - high.astype(jnp.float32)).astype(jnp.bfloat16)
+            got = dot_t(jnp.concatenate([xs, high, low], axis=1), weight_ref[...]).T
+            for t in range(3 * bins):
+                found_ref[t, start : start + group] = got[t * group : (t + 1) * group]
+
+    halves = 2
+    for half in range(halves):
+        span = slice(half * slot_count // halves, (half + 1) * slot_count // halves)
+        last = []
+        mants = []
         expos = []
-        mants = []
         for f in range(bins):
-            pair = white[2 * f * group : 2 * (f + 1) * group]
-            size = jnp.maximum(jnp.abs(pair[:group]), jnp.abs(pair[group:]))
+            gain = lax.rsqrt(jnp.maximum(found_ref[2 * bins + f, span] * (2.0 / band), power_floor))
+            pair = [found_ref[2 * f, span] * gain, found_ref[2 * f + 1, span] * gain]
+            size = jnp.maximum(jnp.abs(pair[0]), jnp.abs(pair[1]))
             peak = jnp.maximum(jnp.max(size, axis=1, keepdims=True), 1e-30)
             expo = jnp.ceil(jnp.log2(peak))
             mant = jnp.floor(peak * jnp.exp2(-expo) * 16384.0) + 1.0
@@ -88,60 +129,41 @@
             expos.append(expo)
             mants.append(mant)
             for p in range(2):
-                q = jnp.round(pair[p * group : (p + 1) * group] * inverse)
-                coded.append(jnp.clip(q, -full, full))
-        for t in range(tail_tile):
-            coded_ref[pl.ds(first, group), t * lanes : (t + 1) * lanes] = coded[t][:, :lanes]
-        last = [c[:, lanes:] for c in coded] + mants + expos + [id_ref[pl.ds(first, group), :]]
+                q = jnp.clip(jnp.round(pair[p] * inverse), -full, full)
+                t = 2 * f + p
+                coded_ref[span, t * lanes : (t + 1) * lanes] = q[:, :lanes]
+                last.append(q[:, lanes:])
+        last += mants + expos + [id_ref[span, :]]
         used = tail_tile * tail + 2 * bins + 1
-        last.append(jnp.zeros((group, lanes - used), jnp.float32))
-        coded_ref[pl.ds(first, group), tail_tile * lanes :] = jnp.concatenate(last, axis=1)
-        return carry
-
-    lax.fori_loop(0, slots_step // group, body, 0)
-
-    @pl.when(step == pl.num_programs(0) - 1)
-    def _():
-        ids = ids_ref[...].astype(jnp.float32)
-        target = jnp.floor((ids + 0.5) * (1.0 / home_rows))
-        shape = (slot_count, slot_count)
-        j = iota(shape, 0)
-        i = iota(shape, 1)
-        target_column = jnp.sum(jnp.where(j == i, target, 0.0), axis=1, keepdims=True)
-        count = count_ref[0]
-        ahead = (j < i) & (j < count) & (target_column == target)
-        within = jnp.sum(jnp.where(ahead, 1.0, 0.0), axis=0, keepdims=True)
-        live = iota((1, slot_count), 1) < count
-        place = jnp.where(live, target * slab + within, -1.0)
-        send_rows = out_ref.shape[0]
-        spot = iota((send_rows, slot_count), 0).astype(jnp.float32)
-        chosen = jnp.where(spot == place, 1.0, 0.0).astype(jnp.bfloat16)
-        high, low = split(coded_ref[...])
-        sent = jnp.dot(chosen, high, preferred_element_type=jnp.float32)
-        sent += jnp.dot(chosen, low, preferred_element_type=jnp.float32)
-        out_ref[...] = sent.astype(jnp.int32).astype(jnp.int16)
+        last.append(jnp.zeros((slot_count // halves, lanes - used), jnp.float32))
+        coded_ref[span, tail_tile * lanes :] = jnp.concatenate(last, axis=1)
+
+    high, low = split(coded_ref[...])
+    sent = jnp.dot(chosen, high, preferred_element_type=jnp.float32)
+    sent += jnp.dot(chosen, low, preferred_element_type=jnp.float32)
+    out_ref[...] = sent.astype(jnp.int32).astype(jnp.int16)
 
 
 def whiten_pack(spectra, station_ids, counts, readers):
     slot_count, segments, two_band = spectra.shape
     home_rows = slot_count // 2
-    slots_step = 32
-    rows = 2 * bins * group
+    parts = (0, 1, 3)
     return pl.pallas_call(
-        functools.partial(whiten_kernel, home_rows),
-        grid=(slot_count // slots_step,),
+        functools.partial(whiten_kernel, home_rows, parts),
         out_shape=jax.ShapeDtypeStruct((readers * slab, width), jnp.int16),
         in_specs=[
             pl.BlockSpec(memory_space=pltpu.SMEM),
-            pl.BlockSpec((1, slot_count), lambda i: (0, 0)),
-            pl.BlockSpec((slots_step, segments, two_band), lambda i: (i, 0, 0)),
+            pl.BlockSpec(memory_space=pltpu.VMEM),
+            pl.BlockSpec(memory_space=pl.ANY),
         ],
-        out_specs=pl.BlockSpec((readers * slab, width), lambda i: (0, 0)),
+        out_specs=pl.BlockSpec(memory_space=pltpu.VMEM),
         scratch_shapes=[
-            pltpu.VMEM((rows, group * two_band), jnp.bfloat16),
-            pltpu.VMEM((rows, group * two_band), jnp.bfloat16),
+            pltpu.VMEM(spectra.shape, spectra.dtype),
+            pltpu.VMEM((lanes, 2 * group * two_band), jnp.bfloat16),
             pltpu.VMEM((slot_count, 1), jnp.float32),
             pltpu.VMEM((slot_count, width), jnp.float32),
+            pltpu.VMEM((3 * bins, slot_count, segments), jnp.float32),
+            pltpu.SemaphoreType.DMA((len(parts) - 1,)),
         ],
         compiler_params=pltpu.CompilerParams(vmem_limit_bytes=vmem_bytes),
         name="whiten_pack",
@@ -169,10 +191,6 @@
         compiler_params=pltpu.CompilerParams(vmem_limit_bytes=vmem_bytes),
         name="settle",
     )(received)
-
-
-def roll(x, shift):
-    return pltpu.roll(x, shift % x.shape[1], 1)
 
 
 def pair_kernel(segments, row_n, col_n, place_ref, *refs):
@@ -274,6 +292,18 @@
     return lax.ppermute(value, axis, [(i, i ^ distance) for i in range(size)])
 
 
+def gather_rows(white, count):
+    blocks = {0: white}
+    distance = 2
+    while distance < count:
+        for k in range(0, distance, 2):
+            blocks[k + distance] = across(blocks[k], "col", distance)
+        distance *= 2
+    for k in range(0, count, 2):
+        blocks[k + 1] = across(blocks[k], "col", 1)
+    return [blocks[k] for k in range(count)]
+
+
 def shards(spectra, station_ids, counts):
     row_count = lax.axis_size("row")
     column_count = lax.axis_size("col")
@@ -283,15 +313,8 @@
     packed = whiten_pack(spectra, station_ids, counts, readers)
     received = lax.all_to_all(packed, ("row", "col"), split_axis=0, concat_axis=0, tiled=True)
     white = settle(received, home_rows, segments)
-    row_blocks = [None] * column_count
-    row_blocks[0] = white
-    col_blocks = [white]
-    for k in range(1, row_count):
-        col_blocks.append(across(white, "row", k))
-    for k in range(2, column_count, 2):
-        row_blocks[k] = across(white, "col", k)
-    for k in range(0, column_count, 2):
-        row_blocks[k + 1] = across(row_blocks[k], "col", 1)
+    row_blocks = gather_rows(white, column_count)
+    col_blocks = [white] + [across(white, "row", k) for k in range(1, row_count)]
     row_index = lax.axis_index("col") ^ jnp.arange(column_count, dtype=jnp.int32)
     col_index = lax.axis_index("row") ^ jnp.arange(row_count, dtype=jnp.int32)
     return pair_tiles(row_blocks, row_index, col_blocks, col_index, segments)

time: 70.3 us -> 59.2 us (0.84)
  blocking collectives: 0 us -> 21.5 us
  starting transfers between devices: 21.2 us -> 6.29 us
  Pallas kernels: 26.9 us -> 15.8 us
  waiting for transfers between devices: 20.5 us -> 14 us
    all_to_all x0 -> x1, blocking collectives: none -> 21.5 us  [shards(): lax.all_to_all(packed, ('row', 'col'), split_axis=0, concat_axis=0, tiled...]
    all_to_all x1 -> x0, waiting for transfers between devices: 14.4 us -> none  [shards(): lax.all_to_all(packed, ('row', 'col'), split_axis=0, concat_axis=0, tiled...]
    pallas_call x1, Pallas kernels: 17.6 us -> 7.18 us  [whiten_pack(): pl.pallas_call(functools.partial(whiten_kernel, home_rows, parts), out_sh...]
    ppermute x10, waiting for transfers between devices: 6.15 us -> 14 us  [across(): return lax.ppermute(value, axis, [(i, i ^ distance) for i in range(size)])]
    ppermute x10, starting transfers between devices: 13.9 us -> 6.29 us  [across(): return lax.ppermute(value, axis, [(i, i ^ distance) for i in range(size)])]
    all_to_all x1 -> x0, starting transfers between devices: 7.3 us -> none  [shards(): lax.all_to_all(packed, ('row', 'col'), split_axis=0, concat_axis=0, tiled...]
  transfers between devices with their start and end apart: 11 -> 10, of which waited for: 4 -> 5; matrix products, arithmetic and copies ran while one was open for 0% -> 0% of each run, Pallas kernels for 0% -> 0%
where the time goes in v2:
time: 59.2 us; the launch traced here: 59 us
  blocking collectives  21.5 us (36%)
  Pallas kernels  15.8 us (27%)
  waiting for transfers between devices  14 us (24%)
  starting transfers between devices  6.29 us (11%)
  between operations  0.7 us (1%)
  local copies, waits for them, and re-layouts  0.68 us (1%)
    all_to_all x1, blocking collectives, shards(): lax.all_to_all(packed, ('row', 'col'), split_axis=0, concat_axis=0, tiled...  21.5 us
    ppermute x10, waiting for transfers between devices, across(): return lax.ppermute(value, axis, [(i, i ^ distance) for i in range(size)])  14 us
    pallas_call x1, Pallas kernels, pair_tiles(): pl.pallas_call(functools.partial(pair_kernel, segments, row_n, col_n), gr...  8.24 us
    pallas_call x1, Pallas kernels, whiten_pack(): pl.pallas_call(functools.partial(whiten_kernel, home_rows, parts), out_sh...  7.18 us
    ppermute x10, starting transfers between devices, across(): return lax.ppermute(value, axis, [(i, i ^ distance) for i in range(size)])  6.29 us
  transfers between devices with their start and end apart: 10, of which 5 were waited for; matrix products, arithmetic and copies ran while one was open for 0% of the time, Pallas kernels for 0%

profile of v2, /device:TPU:0, one launch (start us, length us, event | category | flops | bytes accessed | tf_op | source)
XLA Modules:
  0.0 59.0 jit_solution(7654931143527438122)
XLA Ops:
  0.7 0.7 %copy-done = s32[192]{0:T(256)S(1)} copy-done((s32[192]{0:T(256)S(1)}, s32[192]{0:T(256)}, u32[]{:S(2)}) %copy-start) | copy-done | bytes 792
  1.3 7.2 %whiten_pack.1 = s16[256,896]{1,0:T(8,128)(2,1)S(1)} custom-call(s32[1]{0:T(128)S(6)} %copy.4.count_ref, s32[1,192]{1,0:T(1,128)S(1)} %bitcast.7, bf16[192,144,128]{2,1,0:T(8,128)(2,1)} %source_ref.1), custom_call_target="tpu_custom_call" | custom-call | tf_op jit(solution)/shard_map/whiten_pack/pallas_call | solution.py:151
  8.5 21.5 %all_to_all.11 = s16[32,8,896]{2,1,0:T(8,128)(2,1)S(1)} all-to-all(s16[32,8,896]{2,1,0:T(8,128)(2,1)S(1)} %bitcast.6), channel_id=1, replica_groups=mesh['row'=4,'col'=8] {'row','col'}, dimensions={0} | all-to-all | bytes 917504 | tf_op jit(solution)/shard_map/all_to_all | solution.py:314
  30.0 0.4 settle.1.refs_0_.refs_8_
  30.4 0.8 %collective-permute-start.1 = (s16[96,896]{1,0:T(8,128)(2,1)S(1)}, s16[96,896]{1,0:T(8,128)(2,1)S(1)}, u32[]{:S(2)}, u32[]{:S(2)}) collective-permute-start(s16[96,896]{1,0:T(8,128)(2,1)S(1)} %settle.1.refs_0_.refs_8_), channel_id=1, source_target_pairs={{0,2},{1,3},{2,0},{3,1},{4,6},{5,7},{6,4},{7,5},{8,10},{9,11},{10,... | collective-permute-start | bytes 516104 | tf_op jit(solution)/shard_map/ppermute | solution.py:292
  31.2 1.5 %collective-permute-start.9 = (s16[96,896]{1,0:T(8,128)(2,1)S(1)}, s16[96,896]{1,0:T(8,128)(2,1)S(1)}, u32[]{:S(2)}, u32[]{:S(2)}) collective-permute-start(s16[96,896]{1,0:T(8,128)(2,1)S(1)} %settle.1.refs_0_.refs_8_), channel_id=1, source_target_pairs={{0,24},{8,16},{16,8},{24,0},{1,25},{9,17},{17,9},{25,1},{2,26},{10... | collective-permute-start | bytes 516104 | tf_op jit(solution)/shard_map/ppermute | solution.py:292
  32.6 0.7 %collective-permute-start.8 = (s16[96,896]{1,0:T(8,128)(2,1)S(1)}, s16[96,896]{1,0:T(8,128)(2,1)S(1)}, u32[]{:S(2)}, u32[]{:S(2)}) collective-permute-start(s16[96,896]{1,0:T(8,128)(2,1)S(1)} %settle.1.refs_0_.refs_8_), channel_id=1, source_target_pairs={{0,16},{8,24},{16,0},{24,8},{1,17},{9,25},{17,1},{25,9},{2,18},{10... | collective-permute-start | bytes 516104 | tf_op jit(solution)/shard_map/ppermute | solution.py:292
  33.3 1.0 %collective-permute-start.3 = (s16[96,896]{1,0:T(8,128)(2,1)S(1)}, s16[96,896]{1,0:T(8,128)(2,1)S(1)}, u32[]{:S(2)}, u32[]{:S(2)}) collective-permute-start(s16[96,896]{1,0:T(8,128)(2,1)S(1)} %settle.1.refs_0_.refs_8_), channel_id=1, source_target_pairs={{0,4},{1,5},{2,6},{3,7},{4,0},{5,1},{6,2},{7,3},{8,12},{9,13},{10,... | collective-permute-start | bytes 516104 | tf_op jit(solution)/shard_map/ppermute | solution.py:292
  34.4 2.2 %collective-permute-done.1.refs_2_ = s16[96,896]{1,0:T(8,128)(2,1)S(1)} collective-permute-done((s16[96,896]{1,0:T(8,128)(2,1)S(1)}, s16[96,896]{1,0:T(8,128)(2,1)S(1)}, u32[]{:S(2)}, u32[]{:S(2)}) %collective-permute-start.1) | collective-permute-done | bytes 172064 | tf_op jit(solution)/shard_map/ppermute | solution.py:292
  36.6 0.8 %collective-permute-start.5 = (s16[96,896]{1,0:T(8,128)(2,1)S(1)}, s16[96,896]{1,0:T(8,128)(2,1)S(1)}, u32[]{:S(2)}, u32[]{:S(2)}) collective-permute-start(s16[96,896]{1,0:T(8,128)(2,1)S(1)} %collective-permute-done.1.refs_2_), channel_id=1, source_target_pairs={{0,4},{1,5},{2,6},{3,7},{4,0},{5,1},{6,2},{7,3},{8,12},{9,13},{10,... | collective-permute-start | bytes 516104 | tf_op jit(solution)/shard_map/ppermute | solution.py:292
  37.4 0.9 %collective-permute-start.7 = (s16[96,896]{1,0:T(8,128)(2,1)S(1)}, s16[96,896]{1,0:T(8,128)(2,1)S(1)}, u32[]{:S(2)}, u32[]{:S(2)}) collective-permute-start(s16[96,896]{1,0:T(8,128)(2,1)S(1)} %settle.1.refs_0_.refs_8_), channel_id=1, source_target_pairs={{0,8},{8,0},{16,24},{24,16},{1,9},{9,1},{17,25},{25,17},{2,10},{10... | collective-permute-start | bytes 516104 | tf_op jit(solution)/shard_map/ppermute | solution.py:292
  38.3 2.0 %collective-permute-done.9.refs_11_ = s16[96,896]{1,0:T(8,128)(2,1)S(1)} collective-permute-done((s16[96,896]{1,0:T(8,128)(2,1)S(1)}, s16[96,896]{1,0:T(8,128)(2,1)S(1)}, u32[]{:S(2)}, u32[]{:S(2)}) %collective-permute-start.9) | collective-permute-done | bytes 172064 | tf_op jit(solution)/shard_map/ppermute | solution.py:292
  40.3 0.0 collective-permute-start
  40.3 8.5 %collective-permute-done.8.refs_10_ = s16[96,896]{1,0:T(8,128)(2,1)S(1)} collective-permute-done((s16[96,896]{1,0:T(8,128)(2,1)S(1)}, s16[96,896]{1,0:T(8,128)(2,1)S(1)}, u32[]{:S(2)}, u32[]{:S(2)}) %collective-permute-start.8) | collective-permute-done | bytes 172064 | tf_op jit(solution)/shard_map/ppermute | solution.py:292
  48.8 0.0 collective-permute-start.2
  48.8 0.0 collective-permute-done.3.refs_4_
  48.8 0.5 collective-permute-start.4
  49.3 0.0 collective-permute-done.5.refs_6_
  49.3 0.1 collective-permute-start.6
  49.4 0.0 collective-permute-done.7.refs_9_
  49.4 0.0 collective-permute-done.refs_1_
  49.5 1.0 %collective-permute-done.4.refs_5_ = s16[96,896]{1,0:T(8,128)(2,1)S(1)} collective-permute-done((s16[96,896]{1,0:T(8,128)(2,1)S(1)}, s16[96,896]{1,0:T(8,128)(2,1)S(1)}, u32[]{:S(2)}, u32[]{:S(2)}) %collective-permute-start.4) | collective-permute-done | bytes 172064 | tf_op jit(solution)/shard_map/ppermute | solution.py:292
  50.5 0.3 collective-permute-done.6.refs_7_
  50.8 8.2 %pair_tiles.1 = bf16[3,2,768,384]{3,2,1,0:T(8,128)(2,1)} custom-call(s32[2,8]{1,0:T(2,128)S(1)} %pad_add_fusion.place_ref, s16[96,896]{1,0:T(8,128)(2,1)S(1)} %settle.1.refs_0_.refs_8_, s16[96,896]{1,0:T(8,128)(2,1)S(1)} %collective-permute-done.refs_1_, s16[96,896]{1,0:T(8,128)(2,1)S(1)} %collective-permute-done.1.refs_2_, ...), custom_call_target="tpu_custom_call" | custom-call | tf_op jit(solution)/shard_map/pair_tiles/pallas_call | solution.py:270
  (6 shorter events, 0.0 us)
Async XLA Ops:
  0.7 0.7 %copy-start = (s32[192]{0:T(256)S(1)}, s32[192]{0:T(256)}, u32[]{:S(2)}) copy-start(s32[192]{0:T(256)} %param.4) | copy-start | bytes 2308
  30.4 6.1 %collective-permute-start.1 = (s16[96,896]{1,0:T(8,128)(2,1)S(1)}, s16[96,896]{1,0:T(8,128)(2,1)S(1)}, u32[]{:S(2)}, u32[]{:S(2)}) collective-permute-start(s16[96,896]{1,0:T(8,128)(2,1)S(1)} %settle.1.refs_0_.refs_8_), channel_id=1, source_target_pairs={{0,2},{1,3},{2,0},{3,1},{4,6},{5,7},{6,4},{7,5},{8,10},{9,11},{10,... | collective-permute-start | bytes 516104 | tf_op jit(solution)/shard_map/ppermute | solution.py:292
  31.2 9.1 %collective-permute-start.9 = (s16[96,896]{1,0:T(8,128)(2,1)S(1)}, s16[96,896]{1,0:T(8,128)(2,1)S(1)}, u32[]{:S(2)}, u32[]{:S(2)}) collective-permute-start(s16[96,896]{1,0:T(8,128)(2,1)S(1)} %settle.1.refs_0_.refs_8_), channel_id=1, source_target_pairs={{0,24},{8,16},{16,8},{24,0},{1,25},{9,17},{17,9},{25,1},{2,26},{10... | collective-permute-start | bytes 516104 | tf_op jit(solution)/shard_map/ppermute | solution.py:292
  32.6 16.2 %collective-permute-start.8 = (s16[96,896]{1,0:T(8,128)(2,1)S(1)}, s16[96,896]{1,0:T(8,128)(2,1)S(1)}, u32[]{:S(2)}, u32[]{:S(2)}) collective-permute-start(s16[96,896]{1,0:T(8,128)(2,1)S(1)} %settle.1.refs_0_.refs_8_), channel_id=1, source_target_pairs={{0,16},{8,24},{16,0},{24,8},{1,17},{9,25},{17,1},{25,9},{2,18},{10... | collective-permute-start | bytes 516104 | tf_op jit(solution)/shard_map/ppermute | solution.py:292
  33.3 15.5 %collective-permute-start.3 = (s16[96,896]{1,0:T(8,128)(2,1)S(1)}, s16[96,896]{1,0:T(8,128)(2,1)S(1)}, u32[]{:S(2)}, u32[]{:S(2)}) collective-permute-start(s16[96,896]{1,0:T(8,128)(2,1)S(1)} %settle.1.refs_0_.refs_8_), channel_id=1, source_target_pairs={{0,4},{1,5},{2,6},{3,7},{4,0},{5,1},{6,2},{7,3},{8,12},{9,13},{10,... | collective-permute-start | bytes 516104 | tf_op jit(solution)/shard_map/ppermute | solution.py:292
  36.6 12.8 %collective-permute-start.5 = (s16[96,896]{1,0:T(8,128)(2,1)S(1)}, s16[96,896]{1,0:T(8,128)(2,1)S(1)}, u32[]{:S(2)}, u32[]{:S(2)}) collective-permute-start(s16[96,896]{1,0:T(8,128)(2,1)S(1)} %collective-permute-done.1.refs_2_), channel_id=1, source_target_pairs={{0,4},{1,5},{2,6},{3,7},{4,0},{5,1},{6,2},{7,3},{8,12},{9,13},{10,... | collective-permute-start | bytes 516104 | tf_op jit(solution)/shard_map/ppermute | solution.py:292
  37.4 12.0 %collective-permute-start.7 = (s16[96,896]{1,0:T(8,128)(2,1)S(1)}, s16[96,896]{1,0:T(8,128)(2,1)S(1)}, u32[]{:S(2)}, u32[]{:S(2)}) collective-permute-start(s16[96,896]{1,0:T(8,128)(2,1)S(1)} %settle.1.refs_0_.refs_8_), channel_id=1, source_target_pairs={{0,8},{8,0},{16,24},{24,16},{1,9},{9,1},{17,25},{25,17},{2,10},{10... | collective-permute-start | bytes 516104 | tf_op jit(solution)/shard_map/ppermute | solution.py:292
  40.3 9.2 %collective-permute-start = (s16[96,896]{1,0:T(8,128)(2,1)S(1)}, s16[96,896]{1,0:T(8,128)(2,1)S(1)}, u32[]{:S(2)}, u32[]{:S(2)}) collective-permute-start(s16[96,896]{1,0:T(8,128)(2,1)S(1)} %settle.1.refs_0_.refs_8_), channel_id=1, source_target_pairs={{0,1},{1,0},{2,3},{3,2},{4,5},{5,4},{6,7},{7,6},{8,9},{9,8},{10,11... | collective-permute-start | bytes 516104 | tf_op jit(solution)/shard_map/ppermute | solution.py:292
  48.8 1.7 %collective-permute-start.2 = (s16[96,896]{1,0:T(8,128)(2,1)S(1)}, s16[96,896]{1,0:T(8,128)(2,1)S(1)}, u32[]{:S(2)}, u32[]{:S(2)}) collective-permute-start(s16[96,896]{1,0:T(8,128)(2,1)S(1)} %collective-permute-done.1.refs_2_), channel_id=1, source_target_pairs={{0,1},{1,0},{2,3},{3,2},{4,5},{5,4},{6,7},{7,6},{8,9},{9,8},{10,11... | collective-permute-start | bytes 516104 | tf_op jit(solution)/shard_map/ppermute | solution.py:292
  48.8 1.6 %collective-permute-start.4 = (s16[96,896]{1,0:T(8,128)(2,1)S(1)}, s16[96,896]{1,0:T(8,128)(2,1)S(1)}, u32[]{:S(2)}, u32[]{:S(2)}) collective-permute-start(s16[96,896]{1,0:T(8,128)(2,1)S(1)} %collective-permute-done.3.refs_4_), channel_id=1, source_target_pairs={{0,1},{1,0},{2,3},{3,2},{4,5},{5,4},{6,7},{7,6},{8,9},{9,8},{10,11... | collective-permute-start | bytes 516104 | tf_op jit(solution)/shard_map/ppermute | solution.py:292
  49.3 1.4 %collective-permute-start.6 = (s16[96,896]{1,0:T(8,128)(2,1)S(1)}, s16[96,896]{1,0:T(8,128)(2,1)S(1)}, u32[]{:S(2)}, u32[]{:S(2)}) collective-permute-start(s16[96,896]{1,0:T(8,128)(2,1)S(1)} %collective-permute-done.5.refs_6_), channel_id=1, source_target_pairs={{0,1},{1,0},{2,3},{3,2},{4,5},{5,4},{6,7},{7,6},{8,9},{9,8},{10,11... | collective-permute-start | bytes 516104 | tf_op jit(solution)/shard_map/ppermute | solution.py:292

commit v3 on v2

--- a/solution.py
+++ b/solution.py
@@ -17,6 +17,7 @@
 vmem_bytes = 48 * 1024 * 1024
 
 tail_tile = 2 * bins
+main_width = tail_tile * lanes
 width = (tail_tile + 1) * lanes
 
 
@@ -41,7 +42,7 @@
     return pltpu.roll(x, shift % x.shape[1], 1)
 
 
-def whiten_kernel(home_rows, parts, count_ref, ids_ref, source_ref, out_ref, x_ref, weight_ref, id_ref, coded_ref, found_ref, sems):
+def whiten_kernel(home_rows, parts, count_ref, ids_ref, source_ref, out_ref, x_ref, weight_ref, id_ref, coded_ref, found_ref, stage_ref, ends_ref, sems):
     slot_count, segments, two_band = x_ref.shape
     edges = [slot_count * e // parts[-1] for e in parts]
     copies = []
@@ -141,7 +142,15 @@
     high, low = split(coded_ref[...])
     sent = jnp.dot(chosen, high, preferred_element_type=jnp.float32)
     sent += jnp.dot(chosen, low, preferred_element_type=jnp.float32)
-    out_ref[...] = sent.astype(jnp.int32).astype(jnp.int16)
+    for t in range(tail_tile):
+        stage_ref[t] = sent[:, t * lanes : (t + 1) * lanes]
+    ends_ref[...] = sent[:, main_width:]
+    readers = send_rows // slab
+    for j in range(tail_tile):
+        from_rows = ends_ref[pl.ds(j, readers, stride=slab), :]
+        stage_ref[j, pl.ds(tail_tile, readers, stride=slab), :] = from_rows
+    for t in range(tail_tile):
+        out_ref[:, t * lanes : (t + 1) * lanes] = stage_ref[t].astype(jnp.int32).astype(jnp.int16)
 
 
 def whiten_pack(spectra, station_ids, counts, readers):
@@ -150,7 +159,7 @@
     parts = (0, 1, 3)
     return pl.pallas_call(
         functools.partial(whiten_kernel, home_rows, parts),
-        out_shape=jax.ShapeDtypeStruct((readers * slab, width), jnp.int16),
+        out_shape=jax.ShapeDtypeStruct((readers * slab, main_width), jnp.int16),
         in_specs=[
             pl.BlockSpec(memory_space=pltpu.SMEM),
             pl.BlockSpec(memory_space=pltpu.VMEM),
@@ -163,6 +172,8 @@
             pltpu.VMEM((slot_count, 1), jnp.float32),
             pltpu.VMEM((slot_count, width), jnp.float32),
             pltpu.VMEM((3 * bins, slot_count, segments), jnp.float32),
+            pltpu.VMEM((tail_tile, readers * slab, lanes), jnp.float32),
+            pltpu.VMEM((readers * slab, lanes), jnp.float32),
             pltpu.SemaphoreType.DMA((len(parts) - 1,)),
         ],
         compiler_params=pltpu.CompilerParams(vmem_limit_bytes=vmem_bytes),
@@ -170,126 +181,170 @@
     )(counts, station_ids.reshape(1, slot_count), spectra)
 
 
-def settle_kernel(id_lane, in_ref, out_ref):
+def settle_kernel(id_lane, in_ref, out_ref, stage_ref, ends_ref):
     home_rows = out_ref.shape[0]
-    q = in_ref[...].astype(jnp.int32).astype(jnp.float32)
-    station = q[:, id_lane : id_lane + 1]
-    wanted = (iota((q.shape[0], home_rows), 1) + 1).astype(jnp.float32)
+    rows = in_ref.shape[0]
+    readers = rows // slab
+    for t in range(tail_tile):
+        stage_ref[t] = in_ref[:, t * lanes : (t + 1) * lanes].astype(jnp.int32).astype(jnp.float32)
+    ends_ref[...] = jnp.zeros_like(ends_ref)
+    for j in range(tail_tile):
+        from_rows = stage_ref[j, pl.ds(tail_tile, readers, stride=slab), :]
+        ends_ref[pl.ds(j, readers, stride=slab), :] = from_rows
+    ends = ends_ref[...]
+    station = ends[:, id_lane : id_lane + 1]
+    wanted = (iota((rows, home_rows), 1) + 1).astype(jnp.float32)
     chosen = jnp.where(station == wanted, 1.0, 0.0).astype(jnp.bfloat16)
-    high, low = split(q)
     dims = (((0,), (0,)), ((), ()))
+    high, low = split(jnp.concatenate([stage_ref[t] for t in range(tail_tile)] + [ends], axis=1))
     home = lax.dot_general(chosen, high, dims, preferred_element_type=jnp.float32)
     home += lax.dot_general(chosen, low, dims, preferred_element_type=jnp.float32)
     out_ref[...] = home.astype(jnp.int32).astype(jnp.int16)
 
 
 def settle(received, home_rows, segments):
-    id_lane = tail_tile * lanes + meta_lane(segments) + 2 * bins
     return pl.pallas_call(
-        functools.partial(settle_kernel, id_lane),
+        functools.partial(settle_kernel, meta_lane(segments) + 2 * bins),
         out_shape=jax.ShapeDtypeStruct((home_rows, width), jnp.int16),
+        scratch_shapes=[
+            pltpu.VMEM((tail_tile, received.shape[0], lanes), jnp.float32),
+            pltpu.VMEM((received.shape[0], lanes), jnp.float32),
+        ],
         compiler_params=pltpu.CompilerParams(vmem_limit_bytes=vmem_bytes),
         name="settle",
     )(received)
 
 
-def pair_kernel(segments, row_n, col_n, place_ref, *refs):
+def ends_of(last, f, tail):
+    mine = last if f == 0 else roll(last, -f * 2 * tail)
+    return jnp.where(iota(mine.shape, 1) < 2 * tail, mine, 0.0)
+
+
+def line_up(first, second, third, tail):
+    ending = first.astype(jnp.float32) + roll(second.astype(jnp.float32), 2 * tail)
+    return (ending + roll(third.astype(jnp.float32), 4 * tail)).astype(jnp.bfloat16)
+
+
+def wide(ref, start, size):
+    return ref[:, start : start + size].astype(jnp.int32).astype(jnp.float32)
+
+
+def rows_kernel(segments, row_n, place_ref, *refs):
     row_refs = refs[:row_n]
-    col_refs = refs[row_n : row_n + col_n]
-    out_ref, a_ref, b_ref, scale_ref, tail_ref = refs[row_n + col_n :]
-    f = pl.program_id(0)
+    a_ref, scale_ref = refs[row_n:]
     home_rows = row_refs[0].shape[0]
+    tail = segments - lanes
+    for k in range(row_n):
+        start = pl.multiple_of(place_ref[0, k] * home_rows, home_rows)
+        span = pl.ds(start, home_rows)
+        last = wide(row_refs[k], main_width, lanes)
+        scale_ref[span, :] = last * jnp.exp2(roll(last, -bins)) * (1.0 / (16384.0 * full))
+        for f in range(bins):
+            high, low = split(wide(row_refs[k], 2 * f * lanes, 2 * lanes))
+            tail_high, tail_low = split(ends_of(last, f, tail))
+            ending = line_up(tail_high, tail_low, tail_high, tail)
+            a_ref[f, span, :] = jnp.concatenate([high, low, high, ending], axis=1)
+
+
+def pair_kernel(segments, col_n, place_ref, a_ref, scale_ref, *refs):
+    col_refs = refs[:col_n]
+    out_ref, b_ref, codes_ref, tile_ref, sems = refs[col_n:]
+    home_rows = col_refs[0].shape[0]
     tail = segments - lanes
     meta = meta_lane(segments)
     columns = col_n * home_rows
-    lane = iota((home_rows, lanes), 1)
-    unit = 1.0 / (16384.0 * full)
-
-    def load(ref):
-        start = pl.multiple_of(f * 2 * lanes, 2 * lanes)
-        main = ref[:, pl.ds(start, 2 * lanes)].astype(jnp.int32).astype(jnp.float32)
-        last = ref[:, tail_tile * lanes :].astype(jnp.int32).astype(jnp.float32)
-        mine = pltpu.roll(last, lax.rem(lanes - f * 2 * tail, lanes), 1)
-        return main, last, jnp.where(lane < 2 * tail, mine, 0.0)
-
-    def ends(first, second, third):
-        return first + roll(second, 2 * tail) + roll(third, 4 * tail)
-
-    def wide(x):
-        return x[0].astype(jnp.float32), x[1].astype(jnp.float32)
-
-    for k in range(row_n):
-        main, last, mine = load(row_refs[k])
-        start = pl.multiple_of(place_ref[0, k] * home_rows, home_rows)
-        high, low = split(main)
-        tail_high, tail_low = wide(split(mine))
-        ending = ends(tail_high, tail_low, tail_high).astype(jnp.bfloat16)
-        a_ref[pl.ds(start, home_rows), :] = jnp.concatenate([high, low, high, ending], axis=1)
-        power = last * jnp.exp2(roll(last, -bins))
-        scale = jnp.sum(jnp.where(lane == meta + f, power, 0.0), axis=1, keepdims=True)
-        scale_ref[pl.ds(start, home_rows), :] = scale * unit
-
+    unit = 1.0 / (16384.0 * full * math.sqrt(segments))
+    spans = []
     for k in range(col_n):
-        main, last, mine = load(col_refs[k])
-        turned = jnp.concatenate([-main[:, lanes:], main[:, :lanes]], axis=1)
-        mine_turned = jnp.where(lane < tail, -roll(mine, -tail), roll(mine, tail))
-        mine_turned = jnp.where(lane < 2 * tail, mine_turned, 0.0)
-        start = pl.multiple_of(place_ref[1, k] * home_rows, home_rows)
-        for offset, value, end in ((0, main, mine), (columns, turned, mine_turned)):
-            high, low = split(value)
-            tail_high, tail_low = wide(split(end))
-            ending = ends(tail_high, tail_high, tail_low).astype(jnp.bfloat16)
-            b_ref[pl.ds(offset + start, home_rows), :] = jnp.concatenate([high, high, low, ending], axis=1)
-        tail_ref[pl.ds(start, home_rows), :] = last
-
+        spans.append(pl.multiple_of(place_ref[1, k] * home_rows, home_rows))
+        codes_ref[pl.ds(spans[k], home_rows), :] = wide(col_refs[k], main_width, lanes)
     pick = iota((8, lanes), 0)
-    want = jnp.where(pick == 0, meta + f, meta + bins + f)
-    chosen = jnp.where((iota((8, lanes), 1) == want) & (pick < 2), 1.0, 0.0).astype(jnp.bfloat16)
-    high, low = split(tail_ref[...])
+    chosen = jnp.where((iota((8, lanes), 1) == meta + pick) & (pick < 2 * bins), 1.0, 0.0).astype(jnp.bfloat16)
+    high, low = split(codes_ref[...])
     codes = dot_t(chosen, high) + dot_t(chosen, low)
-    column_scale = codes[0:1] * jnp.exp2(codes[1:2]) * (unit / math.sqrt(segments))
-
-    product = dot_t(a_ref[...], b_ref[...])
-    row_scale = scale_ref[...]
-    for p in range(2):
-        value = product[:, p * columns : (p + 1) * columns] * row_scale * column_scale
-        out_ref[0, p] = value.astype(jnp.bfloat16)
-
-
-def pair_tiles(row_blocks, row_index, col_blocks, col_index, segments):
-    row_n, col_n = len(row_blocks), len(col_blocks)
-    home_rows = row_blocks[0].shape[0]
-    rows, columns = row_n * home_rows, col_n * home_rows
-    most = max(row_n, col_n)
-    place = jnp.stack([
-        jnp.pad(row_index, (0, most - row_n)),
-        jnp.pad(col_index, (0, most - col_n)),
-    ])
-    block = pl.BlockSpec((home_rows, width), lambda f, place: (0, 0))
-    depth = 7 * lanes
+
+    copies = []
+    for f in range(bins):
+        slot = f % 2
+        for k in range(col_n):
+            last = wide(col_refs[k], main_width, lanes)
+            high, low = split(wide(col_refs[k], 2 * f * lanes, 2 * lanes))
+            mine = ends_of(last, f, tail)
+            lane = iota(mine.shape, 1)
+            turned = jnp.where(lane < tail, -roll(mine, -tail), roll(mine, tail))
+            turned = jnp.where(lane < 2 * tail, turned, 0.0)
+            tail_high, tail_low = split(mine)
+            ending = line_up(tail_high, tail_high, tail_low, tail)
+            b_ref[slot, pl.ds(spans[k], home_rows), :] = jnp.concatenate([high, high, low, ending], axis=1)
+            high = jnp.concatenate([-high[:, lanes:], high[:, :lanes]], axis=1)
+            low = jnp.concatenate([-low[:, lanes:], low[:, :lanes]], axis=1)
+            tail_high, tail_low = split(turned)
+            ending = line_up(tail_high, tail_high, tail_low, tail)
+            b_ref[slot, pl.ds(columns + spans[k], home_rows), :] = jnp.concatenate([high, high, low, ending], axis=1)
+        column_scale = codes[f : f + 1] * jnp.exp2(codes[bins + f : bins + f + 1]) * unit
+        row_scale = scale_ref[:, meta + f : meta + f + 1]
+        product = dot_t(a_ref[f], b_ref[slot])
+        for p in range(2):
+            value = product[:, p * columns : (p + 1) * columns] * row_scale * column_scale
+            tile_ref[f, p] = value.astype(jnp.bfloat16)
+        copies.append(pltpu.make_async_copy(tile_ref.at[f], out_ref.at[f], sems.at[f]))
+        copies[f].start()
+    for copy in copies:
+        copy.wait()
+
+
+def prepare_rows(place, row_blocks, segments):
+    row_n = len(row_blocks)
+    rows = row_n * row_blocks[0].shape[0]
+    vmem = pl.BlockSpec(memory_space=pltpu.VMEM)
     return pl.pallas_call(
-        functools.partial(pair_kernel, segments, row_n, col_n),
-        grid_spec=pltpu.PrefetchScalarGridSpec(
-            num_scalar_prefetch=1,
-            grid=(bins,),
-            in_specs=[block] * (row_n + col_n),
-            out_specs=pl.BlockSpec((1, 2, rows, columns), lambda f, place: (f, 0, 0, 0)),
-            scratch_shapes=[
-                pltpu.VMEM((rows, depth), jnp.bfloat16),
-                pltpu.VMEM((2 * columns, depth), jnp.bfloat16),
-                pltpu.VMEM((rows, 1), jnp.float32),
-                pltpu.VMEM((columns, lanes), jnp.float32),
-            ],
+        functools.partial(rows_kernel, segments, row_n),
+        out_shape=(
+            jax.ShapeDtypeStruct((bins, rows, width), jnp.bfloat16),
+            jax.ShapeDtypeStruct((rows, lanes), jnp.float32),
         ),
+        in_specs=[pl.BlockSpec(memory_space=pltpu.SMEM)] + [vmem] * row_n,
+        out_specs=(vmem, vmem),
+        compiler_params=pltpu.CompilerParams(vmem_limit_bytes=vmem_bytes),
+        cost_estimate=pl.CostEstimate(flops=1, bytes_accessed=1, transcendentals=0),
+        name="prepare_rows",
+    )(place, *row_blocks)
+
+
+def pair_tiles(place, row_parts, row_scales, col_blocks, segments):
+    col_n = len(col_blocks)
+    rows = row_scales.shape[0]
+    columns = col_n * col_blocks[0].shape[0]
+    vmem = pl.BlockSpec(memory_space=pltpu.VMEM)
+    return pl.pallas_call(
+        functools.partial(pair_kernel, segments, col_n),
+        in_specs=[pl.BlockSpec(memory_space=pltpu.SMEM)] + [vmem] * (2 + col_n),
+        out_specs=pl.BlockSpec(memory_space=pl.ANY),
+        scratch_shapes=[
+            pltpu.VMEM((2, 2 * columns, width), jnp.bfloat16),
+            pltpu.VMEM((columns, lanes), jnp.float32),
+            pltpu.VMEM((bins, 2, rows, columns), jnp.bfloat16),
+            pltpu.SemaphoreType.DMA((bins,)),
+        ],
         out_shape=jax.ShapeDtypeStruct((bins, 2, rows, columns), jnp.bfloat16),
         compiler_params=pltpu.CompilerParams(vmem_limit_bytes=vmem_bytes),
         name="pair_tiles",
-    )(place, *row_blocks, *col_blocks)
+    )(place, row_parts, row_scales, *col_blocks)
 
 
 def across(value, axis, distance):
     size = lax.axis_size(axis)
     return lax.ppermute(value, axis, [(i, i ^ distance) for i in range(size)])
+
+
+def gather_columns(white, count):
+    blocks = {0: white}
+    distance = count // 2
+    while distance:
+        for k in list(blocks):
+            blocks[k + distance] = across(blocks[k], "row", distance)
+        distance //= 2
+    return [blocks[k] for k in range(count)]
 
 
 def gather_rows(white, count):
@@ -314,10 +369,11 @@
     received = lax.all_to_all(packed, ("row", "col"), split_axis=0, concat_axis=0, tiled=True)
     white = settle(received, home_rows, segments)
     row_blocks = gather_rows(white, column_count)
-    col_blocks = [white] + [across(white, "row", k) for k in range(1, row_count)]
-    row_index = lax.axis_index("col") ^ jnp.arange(column_count, dtype=jnp.int32)
-    col_index = lax.axis_index("row") ^ jnp.arange(row_count, dtype=jnp.int32)
-    return pair_tiles(row_blocks, row_index, col_blocks, col_index, segments)
+    col_blocks = gather_columns(white, row_count)
+    most = jnp.arange(max(row_count, column_count), dtype=jnp.int32)
+    place = jnp.stack([lax.axis_index("col") ^ most, lax.axis_index("row") ^ most])
+    row_parts, row_scales = prepare_rows(place, row_blocks, segments)
+    return pair_tiles(place, row_parts, row_scales, col_blocks, segments)
 
 
 def solution(mesh):

time: 59.2 us -> 54.3 us (0.917)
  waiting for transfers between devices: 14 us -> 11.3 us
  starting transfers between devices: 6.29 us -> 4.85 us
  blocking collectives: 21.5 us -> 20.3 us
    ppermute x10, waiting for transfers between devices: 14 us -> 11.3 us  [across(): return lax.ppermute(value, axis, [(i, i ^ distance) for i in range(size)])]
    ppermute x10, starting transfers between devices: 6.29 us -> 4.85 us  [across(): return lax.ppermute(value, axis, [(i, i ^ distance) for i in range(size)])]
    all_to_all x1, blocking collectives: 21.5 us -> 20.3 us  [shards(): lax.all_to_all(packed, ('row', 'col'), split_axis=0, concat_axis=0, tiled...]
    pallas_call x2 -> x3, Pallas kernels: 8.65 us -> 9.06 us  [the longest x1 6.26 us: pair_tiles(): pl.pallas_call(functools.partial(pair_kernel, segments, col_n), in_specs=...]
  transfers between devices with their start and end apart: 10 -> 10, of which waited for: 5 -> 5; matrix products, arithmetic and copies ran while one was open for 0% -> 0% of each run, Pallas kernels for 0% -> 4%
where the time goes in v3:
time: 54.3 us; the launch traced here: 54.1 us
  blocking collectives  20.3 us (37%)
  Pallas kernels  16.3 us (30%)
  waiting for transfers between devices  11.3 us (21%)
  starting transfers between devices  4.85 us (9%)
  between operations  0.72 us (1%)
  local copies, waits for them, and re-layouts  0.67 us (1%)
    all_to_all x1, blocking collectives, shards(): lax.all_to_all(packed, ('row', 'col'), split_axis=0, concat_axis=0, tiled...  20.3 us
    ppermute x10, waiting for transfers between devices, across(): return lax.ppermute(value, axis, [(i, i ^ distance) for i in range(size)])  11.3 us
    pallas_call x1, Pallas kernels, whiten_pack(): pl.pallas_call(functools.partial(whiten_kernel, home_rows, parts), out_sh...  7.24 us
    pallas_call x1, Pallas kernels, pair_tiles(): pl.pallas_call(functools.partial(pair_kernel, segments, col_n), in_specs=...  6.26 us
    ppermute x10, starting transfers between devices, across(): return lax.ppermute(value, axis, [(i, i ^ distance) for i in range(size)])  4.85 us
    pallas_call x1, Pallas kernels, prepare_rows(): pl.pallas_call(functools.partial(rows_kernel, segments, row_n), out_shape...  2.31 us
  transfers between devices with their start and end apart: 10, of which 5 were waited for; matrix products, arithmetic and copies ran while one was open for 0% of the time, Pallas kernels for 4%

profile of v3, /device:TPU:0, one launch (start us, length us, event | category | flops | bytes accessed | tf_op | source)
XLA Modules:
  0.0 54.1 jit_solution(18356885722551998558)
XLA Ops:
  0.7 0.7 %copy-done = s32[192]{0:T(256)S(1)} copy-done((s32[192]{0:T(256)S(1)}, s32[192]{0:T(256)}, u32[]{:S(2)}) %copy-start) | copy-done | bytes 792
  1.3 7.2 %whiten_pack.1 = s16[256,768]{1,0:T(8,128)(2,1)S(1)} custom-call(s32[1]{0:T(128)S(6)} %copy.4.count_ref, s32[1,192]{1,0:T(1,128)S(1)} %bitcast.5, bf16[192,144,128]{2,1,0:T(8,128)(2,1)} %source_ref.1), custom_call_target="tpu_custom_call" | custom-call | tf_op jit(solution)/shard_map/whiten_pack/pallas_call | solution.py:160
  8.6 20.3 %all_to_all.11 = s16[32,8,768]{2,1,0:T(8,128)(2,1)S(1)} all-to-all(s16[32,8,768]{2,1,0:T(8,128)(2,1)S(1)} %bitcast.3), channel_id=1, replica_groups=mesh['row'=4,'col'=8] {'row','col'}, dimensions={0} | all-to-all | bytes 786432 | tf_op jit(solution)/shard_map/all_to_all | solution.py:369
  28.9 0.5 settle.1.refs_0_
  29.4 0.5 %collective-permute-start.1 = (s16[96,896]{1,0:T(8,128)(2,1)S(1)}, s16[96,896]{1,0:T(8,128)(2,1)S(1)}, u32[]{:S(2)}, u32[]{:S(2)}) collective-permute-start(s16[96,896]{1,0:T(8,128)(2,1)S(1)} %settle.1.refs_0_), channel_id=1, source_target_pairs={{0,2},{1,3},{2,0},{3,1},{4,6},{5,7},{6,4},{7,5},{8,10},{9,11},{10,... | collective-permute-start | bytes 516104 | tf_op jit(solution)/shard_map/ppermute | solution.py:337
  29.9 1.0 %collective-permute-start.8 = (s16[96,896]{1,0:T(8,128)(2,1)S(1)}, s16[96,896]{1,0:T(8,128)(2,1)S(1)}, u32[]{:S(2)}, u32[]{:S(2)}) collective-permute-start(s16[96,896]{1,0:T(8,128)(2,1)S(1)} %settle.1.refs_0_), channel_id=1, source_target_pairs={{0,16},{8,24},{16,0},{24,8},{1,17},{9,25},{17,1},{25,9},{2,18},{10... | collective-permute-start | bytes 516104 | tf_op jit(solution)/shard_map/ppermute | solution.py:337
  30.9 0.6 %collective-permute-start.3 = (s16[96,896]{1,0:T(8,128)(2,1)S(1)}, s16[96,896]{1,0:T(8,128)(2,1)S(1)}, u32[]{:S(2)}, u32[]{:S(2)}) collective-permute-start(s16[96,896]{1,0:T(8,128)(2,1)S(1)} %settle.1.refs_0_), channel_id=1, source_target_pairs={{0,4},{1,5},{2,6},{3,7},{4,0},{5,1},{6,2},{7,3},{8,12},{9,13},{10,... | collective-permute-start | bytes 516104 | tf_op jit(solution)/shard_map/ppermute | solution.py:337
  31.5 0.0 collective-permute-start
  31.5 3.6 %collective-permute-done.1.refs_2_ = s16[96,896]{1,0:T(8,128)(2,1)S(1)} collective-permute-done((s16[96,896]{1,0:T(8,128)(2,1)S(1)}, s16[96,896]{1,0:T(8,128)(2,1)S(1)}, u32[]{:S(2)}, u32[]{:S(2)}) %collective-permute-start.1) | collective-permute-done | bytes 172064 | tf_op jit(solution)/shard_map/ppermute | solution.py:337
  35.2 1.0 %collective-permute-start.5 = (s16[96,896]{1,0:T(8,128)(2,1)S(1)}, s16[96,896]{1,0:T(8,128)(2,1)S(1)}, u32[]{:S(2)}, u32[]{:S(2)}) collective-permute-start(s16[96,896]{1,0:T(8,128)(2,1)S(1)} %collective-permute-done.1.refs_2_), channel_id=1, source_target_pairs={{0,4},{1,5},{2,6},{3,7},{4,0},{5,1},{6,2},{7,3},{8,12},{9,13},{10,... | collective-permute-start | bytes 516104 | tf_op jit(solution)/shard_map/ppermute | solution.py:337
  36.2 1.0 %collective-permute-start.7 = (s16[96,896]{1,0:T(8,128)(2,1)S(1)}, s16[96,896]{1,0:T(8,128)(2,1)S(1)}, u32[]{:S(2)}, u32[]{:S(2)}) collective-permute-start(s16[96,896]{1,0:T(8,128)(2,1)S(1)} %settle.1.refs_0_), channel_id=1, source_target_pairs={{0,8},{8,0},{16,24},{24,16},{1,9},{9,1},{17,25},{25,17},{2,10},{10... | collective-permute-start | bytes 516104 | tf_op jit(solution)/shard_map/ppermute | solution.py:337
  37.2 3.9 %collective-permute-done.8.refs_2_ = s16[96,896]{1,0:T(8,128)(2,1)S(1)} collective-permute-done((s16[96,896]{1,0:T(8,128)(2,1)S(1)}, s16[96,896]{1,0:T(8,128)(2,1)S(1)}, u32[]{:S(2)}, u32[]{:S(2)}) %collective-permute-start.8) | collective-permute-done | bytes 172064 | tf_op jit(solution)/shard_map/ppermute | solution.py:337
  41.1 0.0 collective-permute-start.2
  41.1 0.0 collective-permute-done.3.refs_4_
  41.1 0.6 %collective-permute-start.4 = (s16[96,896]{1,0:T(8,128)(2,1)S(1)}, s16[96,896]{1,0:T(8,128)(2,1)S(1)}, u32[]{:S(2)}, u32[]{:S(2)}) collective-permute-start(s16[96,896]{1,0:T(8,128)(2,1)S(1)} %collective-permute-done.3.refs_4_), channel_id=1, source_target_pairs={{0,1},{1,0},{2,3},{3,2},{4,5},{5,4},{6,7},{7,6},{8,9},{9,8},{10,11... | collective-permute-start | bytes 516104 | tf_op jit(solution)/shard_map/ppermute | solution.py:337
  41.7 0.0 collective-permute-done.5.refs_6_
  41.7 0.1 collective-permute-start.6
  41.8 1.0 %collective-permute-done.4.refs_5_ = s16[96,896]{1,0:T(8,128)(2,1)S(1)} collective-permute-done((s16[96,896]{1,0:T(8,128)(2,1)S(1)}, s16[96,896]{1,0:T(8,128)(2,1)S(1)}, u32[]{:S(2)}, u32[]{:S(2)}) %collective-permute-start.4) | collective-permute-done | bytes 172064 | tf_op jit(solution)/shard_map/ppermute | solution.py:337
  42.7 0.0 collective-permute-done.2.refs_3_
  42.7 0.3 collective-permute-done.6.refs_7_
  43.1 2.3 %prepare_rows.1 = (bf16[3,768,896]{2,1,0:T(8,128)(2,1)S(1)}, f32[768,128]{1,0:T(8,128)S(1)}) custom-call(s32[2,8]{1,0:T(2,128)S(1)} %pad_add_fusion.place_ref, s16[96,896]{1,0:T(8,128)(2,1)S(1)} %settle.1.refs_0_, s16[96,896]{1,0:T(8,128)(2,1)S(1)} %collective-permute-done.refs_1_, s16[96,896]{1,0:T(8,128)(2,1)S(1)} %collective-permute-done.1.refs_2_, ...), custom_call_target="tpu_custom_call" | custom-call | flops 1 | bytes 1 | tf_op jit(solution)/shard_map/prepare_rows/pallas_call | solution.py:300
  45.4 0.0 collective-permute-done.7.refs_1_
  45.4 2.5 %collective-permute-done.9.refs_3_ = s16[96,896]{1,0:T(8,128)(2,1)S(1)} collective-permute-done((s16[96,896]{1,0:T(8,128)(2,1)S(1)}, s16[96,896]{1,0:T(8,128)(2,1)S(1)}, u32[]{:S(2)}, u32[]{:S(2)}) %collective-permute-start.9) | collective-permute-done | bytes 172064 | tf_op jit(solution)/shard_map/ppermute | solution.py:337
  47.9 6.3 %pair_tiles.1 = bf16[3,2,768,384]{3,2,1,0:T(8,128)(2,1)} custom-call(s32[2,8]{1,0:T(2,128)S(1)} %pad_add_fusion.place_ref, bf16[3,768,896]{2,1,0:T(8,128)(2,1)S(1)} %get-tuple-element.7.a_ref, f32[768,128]{1,0:T(8,128)S(1)} %get-tuple-element.8.scale_ref, s16[96,896]{1,0:T(8,128)(2,1)S(1)} %settle.1.refs_0_, ...), custom_call_target="tpu_custom_call" | custom-call | tf_op jit(solution)/shard_map/pair_tiles/pallas_call | solution.py:319
  (5 shorter events, 0.0 us)
Async XLA Ops:
  0.7 0.7 %copy-start = (s32[192]{0:T(256)S(1)}, s32[192]{0:T(256)}, u32[]{:S(2)}) copy-start(s32[192]{0:T(256)} %param.4) | copy-start | bytes 2308
  29.4 5.8 %collective-permute-start.1 = (s16[96,896]{1,0:T(8,128)(2,1)S(1)}, s16[96,896]{1,0:T(8,128)(2,1)S(1)}, u32[]{:S(2)}, u32[]{:S(2)}) collective-permute-start(s16[96,896]{1,0:T(8,128)(2,1)S(1)} %settle.1.refs_0_), channel_id=1, source_target_pairs={{0,2},{1,3},{2,0},{3,1},{4,6},{5,7},{6,4},{7,5},{8,10},{9,11},{10,... | collective-permute-start | bytes 516104 | tf_op jit(solution)/shard_map/ppermute | solution.py:337
  29.9 11.2 %collective-permute-start.8 = (s16[96,896]{1,0:T(8,128)(2,1)S(1)}, s16[96,896]{1,0:T(8,128)(2,1)S(1)}, u32[]{:S(2)}, u32[]{:S(2)}) collective-permute-start(s16[96,896]{1,0:T(8,128)(2,1)S(1)} %settle.1.refs_0_), channel_id=1, source_target_pairs={{0,16},{8,24},{16,0},{24,8},{1,17},{9,25},{17,1},{25,9},{2,18},{10... | collective-permute-start | bytes 516104 | tf_op jit(solution)/shard_map/ppermute | solution.py:337
  30.9 10.1 %collective-permute-start.3 = (s16[96,896]{1,0:T(8,128)(2,1)S(1)}, s16[96,896]{1,0:T(8,128)(2,1)S(1)}, u32[]{:S(2)}, u32[]{:S(2)}) collective-permute-start(s16[96,896]{1,0:T(8,128)(2,1)S(1)} %settle.1.refs_0_), channel_id=1, source_target_pairs={{0,4},{1,5},{2,6},{3,7},{4,0},{5,1},{6,2},{7,3},{8,12},{9,13},{10,... | collective-permute-start | bytes 516104 | tf_op jit(solution)/shard_map/ppermute | solution.py:337
  31.5 9.6 %collective-permute-start = (s16[96,896]{1,0:T(8,128)(2,1)S(1)}, s16[96,896]{1,0:T(8,128)(2,1)S(1)}, u32[]{:S(2)}, u32[]{:S(2)}) collective-permute-start(s16[96,896]{1,0:T(8,128)(2,1)S(1)} %settle.1.refs_0_), channel_id=1, source_target_pairs={{0,1},{1,0},{2,3},{3,2},{4,5},{5,4},{6,7},{7,6},{8,9},{9,8},{10,11... | collective-permute-start | bytes 516104 | tf_op jit(solution)/shard_map/ppermute | solution.py:337
  35.2 6.5 %collective-permute-start.5 = (s16[96,896]{1,0:T(8,128)(2,1)S(1)}, s16[96,896]{1,0:T(8,128)(2,1)S(1)}, u32[]{:S(2)}, u32[]{:S(2)}) collective-permute-start(s16[96,896]{1,0:T(8,128)(2,1)S(1)} %collective-permute-done.1.refs_2_), channel_id=1, source_target_pairs={{0,4},{1,5},{2,6},{3,7},{4,0},{5,1},{6,2},{7,3},{8,12},{9,13},{10,... | collective-permute-start | bytes 516104 | tf_op jit(solution)/shard_map/ppermute | solution.py:337
  36.2 9.2 %collective-permute-start.7 = (s16[96,896]{1,0:T(8,128)(2,1)S(1)}, s16[96,896]{1,0:T(8,128)(2,1)S(1)}, u32[]{:S(2)}, u32[]{:S(2)}) collective-permute-start(s16[96,896]{1,0:T(8,128)(2,1)S(1)} %settle.1.refs_0_), channel_id=1, source_target_pairs={{0,8},{8,0},{16,24},{24,16},{1,9},{9,1},{17,25},{25,17},{2,10},{10... | collective-permute-start | bytes 516104 | tf_op jit(solution)/shard_map/ppermute | solution.py:337
  41.1 1.7 %collective-permute-start.2 = (s16[96,896]{1,0:T(8,128)(2,1)S(1)}, s16[96,896]{1,0:T(8,128)(2,1)S(1)}, u32[]{:S(2)}, u32[]{:S(2)}) collective-permute-start(s16[96,896]{1,0:T(8,128)(2,1)S(1)} %collective-permute-done.1.refs_2_), channel_id=1, source_target_pairs={{0,1},{1,0},{2,3},{3,2},{4,5},{5,4},{6,7},{7,6},{8,9},{9,8},{10,11... | collective-permute-start | bytes 516104 | tf_op jit(solution)/shard_map/ppermute | solution.py:337
  41.1 6.8 %collective-permute-start.9 = (s16[96,896]{1,0:T(8,128)(2,1)S(1)}, s16[96,896]{1,0:T(8,128)(2,1)S(1)}, u32[]{:S(2)}, u32[]{:S(2)}) collective-permute-start(s16[96,896]{1,0:T(8,128)(2,1)S(1)} %collective-permute-done.8.refs_2_), channel_id=1, source_target_pairs={{0,8},{8,0},{16,24},{24,16},{1,9},{9,1},{17,25},{25,17},{2,10},{10... | collective-permute-start | bytes 516104 | tf_op jit(solution)/shard_map/ppermute | solution.py:337
  41.1 1.6 %collective-permute-start.4 = (s16[96,896]{1,0:T(8,128)(2,1)S(1)}, s16[96,896]{1,0:T(8,128)(2,1)S(1)}, u32[]{:S(2)}, u32[]{:S(2)}) collective-permute-start(s16[96,896]{1,0:T(8,128)(2,1)S(1)} %collective-permute-done.3.refs_4_), channel_id=1, source_target_pairs={{0,1},{1,0},{2,3},{3,2},{4,5},{5,4},{6,7},{7,6},{8,9},{9,8},{10,11... | collective-permute-start | bytes 516104 | tf_op jit(solution)/shard_map/ppermute | solution.py:337
  41.7 1.4 %collective-permute-start.6 = (s16[96,896]{1,0:T(8,128)(2,1)S(1)}, s16[96,896]{1,0:T(8,128)(2,1)S(1)}, u32[]{:S(2)}, u32[]{:S(2)}) collective-permute-start(s16[96,896]{1,0:T(8,128)(2,1)S(1)} %collective-permute-done.5.refs_6_), channel_id=1, source_target_pairs={{0,1},{1,0},{2,3},{3,2},{4,5},{5,4},{6,7},{7,6},{8,9},{9,8},{10,11... | collective-permute-start | bytes 516104 | tf_op jit(solution)/shard_map/ppermute | solution.py:337

commit v4 on v3

--- a/solution.py
+++ b/solution.py
@@ -101,11 +101,11 @@
             xs = jnp.concatenate([x[s] for s in range(group)], axis=1)
             folded = []
             for s in range(0, group, 2):
-                pair = []
-                for xf in (x[s].astype(jnp.float32), x[s + 1].astype(jnp.float32)):
-                    energy = xf * xf
-                    pair.append(energy + roll(energy, band))
-                folded.append(jnp.where(left, pair[0], pair[1]))
+                first = x[s]
+                second = x[s + 1]
+                near = jnp.concatenate([first[:, :band], second[:, band:]], axis=1).astype(jnp.float32)
+                far = jnp.concatenate([first[:, band:], second[:, :band]], axis=1).astype(jnp.float32)
+                folded.append(near * near + far * far)
             folded = jnp.concatenate(folded, axis=1)
             high = folded.astype(jnp.bfloat16)
             low = (folded - high.astype(jnp.float32)).astype(jnp.bfloat16)
@@ -332,6 +332,25 @@
     )(place, row_parts, row_scales, *col_blocks)
 
 
+def copy_kernel(in_ref, out_ref):
+    out_ref[...] = in_ref[...]
+
+
+def copy_block(block, weight):
+    vmem = pl.BlockSpec(memory_space=pltpu.VMEM)
+    if weight == 0:
+        return block
+    return pl.pallas_call(
+        copy_kernel,
+        out_shape=jax.ShapeDtypeStruct(block.shape, block.dtype),
+        in_specs=[vmem],
+        out_specs=vmem,
+        compiler_params=pltpu.CompilerParams(vmem_limit_bytes=vmem_bytes),
+        cost_estimate=pl.CostEstimate(flops=weight * 2 * 10**9, bytes_accessed=10**5, transcendentals=0),
+        name="copy_block",
+    )(block)
+
+
 def across(value, axis, distance):
     size = lax.axis_size(axis)
     return lax.ppermute(value, axis, [(i, i ^ distance) for i in range(size)])
@@ -342,7 +361,7 @@
     distance = count // 2
     while distance:
         for k in list(blocks):
-            blocks[k + distance] = across(blocks[k], "row", distance)
+            blocks[k + distance] = across(copy_block(blocks[k], 1) if k and distance == 1 else blocks[k], "row", distance)
         distance //= 2
     return [blocks[k] for k in range(count)]
 

time: 54.3 us -> 53.2 us (0.980)
  waiting for transfers between devices: 11.3 us -> 9.74 us
  starting transfers between devices: 4.85 us -> 5.73 us
    ppermute x10, waiting for transfers between devices: 11.3 us -> 9.74 us  [across(): return lax.ppermute(value, axis, [(i, i ^ distance) for i in range(size)])]
    ppermute x10, starting transfers between devices: 4.85 us -> 5.73 us  [across(): return lax.ppermute(value, axis, [(i, i ^ distance) for i in range(size)])]
where the time goes in v4:
time: 53.2 us; the launch traced here: 53 us
  blocking collectives  20.3 us (38%)
  Pallas kernels  15.9 us (30%)
  waiting for transfers between devices  9.74 us (18%)
  starting transfers between devices  5.73 us (11%)
  between operations  0.73 us (1%)
  local copies, waits for them, and re-layouts  0.67 us (1%)
    all_to_all x1, blocking collectives, shards(): lax.all_to_all(packed, ('row', 'col'), split_axis=0, concat_axis=0, tiled...  20.3 us
    ppermute x10, waiting for transfers between devices, across(): return lax.ppermute(value, axis, [(i, i ^ distance) for i in range(size)])  9.74 us
    pallas_call x1, Pallas kernels, whiten_pack(): pl.pallas_call(functools.partial(whiten_kernel, home_rows, parts), out_sh...  6.8 us
    pallas_call x1, Pallas kernels, pair_tiles(): pl.pallas_call(functools.partial(pair_kernel, segments, col_n), in_specs=...  6.26 us
    ppermute x10, starting transfers between devices, across(): return lax.ppermute(value, axis, [(i, i ^ distance) for i in range(size)])  5.73 us
    pallas_call x1, Pallas kernels, prepare_rows(): pl.pallas_call(functools.partial(rows_kernel, segments, row_n), out_shape...  2.3 us
  transfers between devices with their start and end apart: 10, of which 5 were waited for; matrix products, arithmetic and copies ran while one was open for 0% of the time, Pallas kernels for 4%

profile of v4, /device:TPU:0, one launch (start us, length us, event | category | flops | bytes accessed | tf_op | source)
XLA Modules:
  0.0 53.0 jit_solution(10632955090504470847)
XLA Ops:
  0.7 0.7 %copy-done = s32[192]{0:T(256)S(1)} copy-done((s32[192]{0:T(256)S(1)}, s32[192]{0:T(256)}, u32[]{:S(2)}) %copy-start) | copy-done | bytes 792
  1.3 6.8 %whiten_pack.1 = s16[256,768]{1,0:T(8,128)(2,1)S(1)} custom-call(s32[1]{0:T(128)S(6)} %copy.4.count_ref, s32[1,192]{1,0:T(1,128)S(1)} %bitcast.5, bf16[192,144,128]{2,1,0:T(8,128)(2,1)} %source_ref.1), custom_call_target="tpu_custom_call" | custom-call | tf_op jit(solution)/shard_map/whiten_pack/pallas_call | solution.py:160
  8.1 20.3 %all_to_all.11 = s16[32,8,768]{2,1,0:T(8,128)(2,1)S(1)} all-to-all(s16[32,8,768]{2,1,0:T(8,128)(2,1)S(1)} %bitcast.3), channel_id=1, replica_groups=mesh['row'=4,'col'=8] {'row','col'}, dimensions={0} | all-to-all | bytes 786432 | tf_op jit(solution)/shard_map/all_to_all | solution.py:388
  28.4 0.5 settle.1.refs_0_
  28.9 0.5 %collective-permute-start.1 = (s16[96,896]{1,0:T(8,128)(2,1)S(1)}, s16[96,896]{1,0:T(8,128)(2,1)S(1)}, u32[]{:S(2)}, u32[]{:S(2)}) collective-permute-start(s16[96,896]{1,0:T(8,128)(2,1)S(1)} %settle.1.refs_0_), channel_id=1, source_target_pairs={{0,2},{1,3},{2,0},{3,1},{4,6},{5,7},{6,4},{7,5},{8,10},{9,11},{10,... | collective-permute-start | bytes 516104 | tf_op jit(solution)/shard_map/ppermute | solution.py:356
  29.5 1.0 %collective-permute-start.8 = (s16[96,896]{1,0:T(8,128)(2,1)S(1)}, s16[96,896]{1,0:T(8,128)(2,1)S(1)}, u32[]{:S(2)}, u32[]{:S(2)}) collective-permute-start(s16[96,896]{1,0:T(8,128)(2,1)S(1)} %settle.1.refs_0_), channel_id=1, source_target_pairs={{0,16},{8,24},{16,0},{24,8},{1,17},{9,25},{17,1},{25,9},{2,18},{10... | collective-permute-start | bytes 516104 | tf_op jit(solution)/shard_map/ppermute | solution.py:356
  30.5 1.0 %collective-permute-start.7 = (s16[96,896]{1,0:T(8,128)(2,1)S(1)}, s16[96,896]{1,0:T(8,128)(2,1)S(1)}, u32[]{:S(2)}, u32[]{:S(2)}) collective-permute-start(s16[96,896]{1,0:T(8,128)(2,1)S(1)} %settle.1.refs_0_), channel_id=1, source_target_pairs={{0,8},{8,0},{16,24},{24,16},{1,9},{9,1},{17,25},{25,17},{2,10},{10... | collective-permute-start | bytes 516104 | tf_op jit(solution)/shard_map/ppermute | solution.py:356
  31.5 1.5 %collective-permute-start.3 = (s16[96,896]{1,0:T(8,128)(2,1)S(1)}, s16[96,896]{1,0:T(8,128)(2,1)S(1)}, u32[]{:S(2)}, u32[]{:S(2)}) collective-permute-start(s16[96,896]{1,0:T(8,128)(2,1)S(1)} %settle.1.refs_0_), channel_id=1, source_target_pairs={{0,4},{1,5},{2,6},{3,7},{4,0},{5,1},{6,2},{7,3},{8,12},{9,13},{10,... | collective-permute-start | bytes 516104 | tf_op jit(solution)/shard_map/ppermute | solution.py:356
  32.9 0.0 collective-permute-start
  32.9 1.8 %collective-permute-done.1.refs_2_ = s16[96,896]{1,0:T(8,128)(2,1)S(1)} collective-permute-done((s16[96,896]{1,0:T(8,128)(2,1)S(1)}, s16[96,896]{1,0:T(8,128)(2,1)S(1)}, u32[]{:S(2)}, u32[]{:S(2)}) %collective-permute-start.1) | collective-permute-done | bytes 172064 | tf_op jit(solution)/shard_map/ppermute | solution.py:356
  34.7 1.0 %collective-permute-start.5 = (s16[96,896]{1,0:T(8,128)(2,1)S(1)}, s16[96,896]{1,0:T(8,128)(2,1)S(1)}, u32[]{:S(2)}, u32[]{:S(2)}) collective-permute-start(s16[96,896]{1,0:T(8,128)(2,1)S(1)} %collective-permute-done.1.refs_2_), channel_id=1, source_target_pairs={{0,4},{1,5},{2,6},{3,7},{4,0},{5,1},{6,2},{7,3},{8,12},{9,13},{10,... | collective-permute-start | bytes 516104 | tf_op jit(solution)/shard_map/ppermute | solution.py:356
  35.7 4.8 %collective-permute-done.8.in_ref.refs_2_ = s16[96,896]{1,0:T(8,128)(2,1)S(1)} collective-permute-done((s16[96,896]{1,0:T(8,128)(2,1)S(1)}, s16[96,896]{1,0:T(8,128)(2,1)S(1)}, u32[]{:S(2)}, u32[]{:S(2)}) %collective-permute-start.8) | collective-permute-done | bytes 172064 | tf_op jit(solution)/shard_map/ppermute | solution.py:356
  40.6 0.1 collective-permute-start.9
  40.6 0.0 collective-permute-done.3.refs_4_
  40.6 0.1 collective-permute-start.2
  40.7 0.0 collective-permute-done.refs_1_
  40.7 0.5 collective-permute-start.4
  41.2 0.1 collective-permute-start.6
  41.3 1.0 %collective-permute-done.4.refs_5_ = s16[96,896]{1,0:T(8,128)(2,1)S(1)} collective-permute-done((s16[96,896]{1,0:T(8,128)(2,1)S(1)}, s16[96,896]{1,0:T(8,128)(2,1)S(1)}, u32[]{:S(2)}, u32[]{:S(2)}) %collective-permute-start.4) | collective-permute-done | bytes 172064 | tf_op jit(solution)/shard_map/ppermute | solution.py:356
  42.4 0.3 collective-permute-done.6.refs_7_
  42.6 2.3 %prepare_rows.1 = (bf16[3,768,896]{2,1,0:T(8,128)(2,1)S(1)}, f32[768,128]{1,0:T(8,128)S(1)}) custom-call(s32[2,8]{1,0:T(2,128)S(1)} %pad_add_fusion.place_ref, s16[96,896]{1,0:T(8,128)(2,1)S(1)} %settle.1.refs_0_, s16[96,896]{1,0:T(8,128)(2,1)S(1)} %collective-permute-done.refs_1_, s16[96,896]{1,0:T(8,128)(2,1)S(1)} %collective-permute-done.1.refs_2_, ...), custom_call_target="tpu_custom_call" | custom-call | flops 1 | bytes 1 | tf_op jit(solution)/shard_map/prepare_rows/pallas_call | solution.py:300
  44.9 0.0 collective-permute-done.7.refs_1_
  45.0 1.8 %collective-permute-done.9.refs_3_ = s16[96,896]{1,0:T(8,128)(2,1)S(1)} collective-permute-done((s16[96,896]{1,0:T(8,128)(2,1)S(1)}, s16[96,896]{1,0:T(8,128)(2,1)S(1)}, u32[]{:S(2)}, u32[]{:S(2)}) %collective-permute-start.9) | collective-permute-done | bytes 172064 | tf_op jit(solution)/shard_map/ppermute | solution.py:356
  46.8 6.3 %pair_tiles.1 = bf16[3,2,768,384]{3,2,1,0:T(8,128)(2,1)} custom-call(s32[2,8]{1,0:T(2,128)S(1)} %pad_add_fusion.place_ref, bf16[3,768,896]{2,1,0:T(8,128)(2,1)S(1)} %get-tuple-element.7.a_ref, f32[768,128]{1,0:T(8,128)S(1)} %get-tuple-element.8.scale_ref, s16[96,896]{1,0:T(8,128)(2,1)S(1)} %settle.1.refs_0_, ...), custom_call_target="tpu_custom_call" | custom-call | tf_op jit(solution)/shard_map/pair_tiles/pallas_call | solution.py:319
  (6 shorter events, 0.0 us)
Async XLA Ops:
  0.7 0.7 %copy-start = (s32[192]{0:T(256)S(1)}, s32[192]{0:T(256)}, u32[]{:S(2)}) copy-start(s32[192]{0:T(256)} %param.4) | copy-start | bytes 2308
  28.9 5.8 %collective-permute-start.1 = (s16[96,896]{1,0:T(8,128)(2,1)S(1)}, s16[96,896]{1,0:T(8,128)(2,1)S(1)}, u32[]{:S(2)}, u32[]{:S(2)}) collective-permute-start(s16[96,896]{1,0:T(8,128)(2,1)S(1)} %settle.1.refs_0_), channel_id=1, source_target_pairs={{0,2},{1,3},{2,0},{3,1},{4,6},{5,7},{6,4},{7,5},{8,10},{9,11},{10,... | collective-permute-start | bytes 516104 | tf_op jit(solution)/shard_map/ppermute | solution.py:356
  29.5 11.1 %collective-permute-start.8 = (s16[96,896]{1,0:T(8,128)(2,1)S(1)}, s16[96,896]{1,0:T(8,128)(2,1)S(1)}, u32[]{:S(2)}, u32[]{:S(2)}) collective-permute-start(s16[96,896]{1,0:T(8,128)(2,1)S(1)} %settle.1.refs_0_), channel_id=1, source_target_pairs={{0,16},{8,24},{16,0},{24,8},{1,17},{9,25},{17,1},{25,9},{2,18},{10... | collective-permute-start | bytes 516104 | tf_op jit(solution)/shard_map/ppermute | solution.py:356
  30.5 14.4 %collective-permute-start.7 = (s16[96,896]{1,0:T(8,128)(2,1)S(1)}, s16[96,896]{1,0:T(8,128)(2,1)S(1)}, u32[]{:S(2)}, u32[]{:S(2)}) collective-permute-start(s16[96,896]{1,0:T(8,128)(2,1)S(1)} %settle.1.refs_0_), channel_id=1, source_target_pairs={{0,8},{8,0},{16,24},{24,16},{1,9},{9,1},{17,25},{25,17},{2,10},{10... | collective-permute-start | bytes 516104 | tf_op jit(solution)/shard_map/ppermute | solution.py:356
  31.5 9.1 %collective-permute-start.3 = (s16[96,896]{1,0:T(8,128)(2,1)S(1)}, s16[96,896]{1,0:T(8,128)(2,1)S(1)}, u32[]{:S(2)}, u32[]{:S(2)}) collective-permute-start(s16[96,896]{1,0:T(8,128)(2,1)S(1)} %settle.1.refs_0_), channel_id=1, source_target_pairs={{0,4},{1,5},{2,6},{3,7},{4,0},{5,1},{6,2},{7,3},{8,12},{9,13},{10,... | collective-permute-start | bytes 516104 | tf_op jit(solution)/shard_map/ppermute | solution.py:356
  32.9 7.8 %collective-permute-start = (s16[96,896]{1,0:T(8,128)(2,1)S(1)}, s16[96,896]{1,0:T(8,128)(2,1)S(1)}, u32[]{:S(2)}, u32[]{:S(2)}) collective-permute-start(s16[96,896]{1,0:T(8,128)(2,1)S(1)} %settle.1.refs_0_), channel_id=1, source_target_pairs={{0,1},{1,0},{2,3},{3,2},{4,5},{5,4},{6,7},{7,6},{8,9},{9,8},{10,11... | collective-permute-start | bytes 516104 | tf_op jit(solution)/shard_map/ppermute | solution.py:356
  34.7 6.5 %collective-permute-start.5 = (s16[96,896]{1,0:T(8,128)(2,1)S(1)}, s16[96,896]{1,0:T(8,128)(2,1)S(1)}, u32[]{:S(2)}, u32[]{:S(2)}) collective-permute-start(s16[96,896]{1,0:T(8,128)(2,1)S(1)} %collective-permute-done.1.refs_2_), channel_id=1, source_target_pairs={{0,4},{1,5},{2,6},{3,7},{4,0},{5,1},{6,2},{7,3},{8,12},{9,13},{10,... | collective-permute-start | bytes 516104 | tf_op jit(solution)/shard_map/ppermute | solution.py:356
  40.6 6.2 %collective-permute-start.9 = (s16[96,896]{1,0:T(8,128)(2,1)S(1)}, s16[96,896]{1,0:T(8,128)(2,1)S(1)}, u32[]{:S(2)}, u32[]{:S(2)}) collective-permute-start(s16[96,896]{1,0:T(8,128)(2,1)S(1)} %copy_block.1), channel_id=1, source_target_pairs={{0,8},{8,0},{16,24},{24,16},{1,9},{9,1},{17,25},{25,17},{2,10},{10... | collective-permute-start | bytes 516104 | tf_op jit(solution)/shard_map/ppermute | solution.py:356
  40.6 1.7 %collective-permute-start.2 = (s16[96,896]{1,0:T(8,128)(2,1)S(1)}, s16[96,896]{1,0:T(8,128)(2,1)S(1)}, u32[]{:S(2)}, u32[]{:S(2)}) collective-permute-start(s16[96,896]{1,0:T(8,128)(2,1)S(1)} %collective-permute-done.1.refs_2_), channel_id=1, source_target_pairs={{0,1},{1,0},{2,3},{3,2},{4,5},{5,4},{6,7},{7,6},{8,9},{9,8},{10,11... | collective-permute-start | bytes 516104 | tf_op jit(solution)/shard_map/ppermute | solution.py:356
  40.7 1.6 %collective-permute-start.4 = (s16[96,896]{1,0:T(8,128)(2,1)S(1)}, s16[96,896]{1,0:T(8,128)(2,1)S(1)}, u32[]{:S(2)}, u32[]{:S(2)}) collective-permute-start(s16[96,896]{1,0:T(8,128)(2,1)S(1)} %collective-permute-done.3.refs_4_), channel_id=1, source_target_pairs={{0,1},{1,0},{2,3},{3,2},{4,5},{5,4},{6,7},{7,6},{8,9},{9,8},{10,11... | collective-permute-start | bytes 516104 | tf_op jit(solution)/shard_map/ppermute | solution.py:356
  41.2 1.4 %collective-permute-start.6 = (s16[96,896]{1,0:T(8,128)(2,1)S(1)}, s16[96,896]{1,0:T(8,128)(2,1)S(1)}, u32[]{:S(2)}, u32[]{:S(2)}) collective-permute-start(s16[96,896]{1,0:T(8,128)(2,1)S(1)} %collective-permute-done.5.refs_6_), channel_id=1, source_target_pairs={{0,1},{1,0},{2,3},{3,2},{4,5},{5,4},{6,7},{7,6},{8,9},{9,8},{10,11... | collective-permute-start | bytes 516104 | tf_op jit(solution)/shard_map/ppermute | solution.py:356

commit v5 on v4

--- a/solution.py
+++ b/solution.py
@@ -42,7 +42,7 @@
     return pltpu.roll(x, shift % x.shape[1], 1)
 
 
-def whiten_kernel(home_rows, parts, count_ref, ids_ref, source_ref, out_ref, x_ref, weight_ref, id_ref, coded_ref, found_ref, stage_ref, ends_ref, sems):
+def whiten_kernel(home_rows, row_count, column_count, parts, count_ref, ids_ref, source_ref, out_ref, x_ref, weight_ref, id_ref, coded_ref, found_ref, stage_ref, ends_ref, sems):
     slot_count, segments, two_band = x_ref.shape
     edges = [slot_count * e // parts[-1] for e in parts]
     copies = []
@@ -89,7 +89,12 @@
     ahead = (j < i) & (j < count) & (target_column == target)
     within = jnp.sum(jnp.where(ahead, 1.0, 0.0), axis=0, keepdims=True)
     live = iota((1, slot_count), 1) < count
-    place = jnp.where(live, target * slab + within, -1.0)
+    row_of = jnp.floor((target + 0.5) * (1.0 / column_count))
+    column_of = target - row_of * column_count
+    half_of = jnp.floor((column_of + 0.5) * 0.5)
+    core_of = column_of - 2.0 * half_of
+    peer = (core_of * (column_count // 2) + half_of) * row_count + row_of
+    place = jnp.where(live, peer * slab + within, -1.0)
     send_rows = out_ref.shape[0]
     spot = iota((send_rows, slot_count), 0).astype(jnp.float32)
     chosen = jnp.where(spot == place, 1.0, 0.0).astype(jnp.bfloat16)
@@ -153,12 +158,13 @@
         out_ref[:, t * lanes : (t + 1) * lanes] = stage_ref[t].astype(jnp.int32).astype(jnp.int16)
 
 
-def whiten_pack(spectra, station_ids, counts, readers):
+def whiten_pack(spectra, station_ids, counts, row_count, column_count):
+    readers = row_count * column_count
     slot_count, segments, two_band = spectra.shape
     home_rows = slot_count // 2
     parts = (0, 1, 3)
     return pl.pallas_call(
-        functools.partial(whiten_kernel, home_rows, parts),
+        functools.partial(whiten_kernel, home_rows, row_count, column_count, parts),
         out_shape=jax.ShapeDtypeStruct((readers * slab, main_width), jnp.int16),
         in_specs=[
             pl.BlockSpec(memory_space=pltpu.SMEM),
@@ -381,11 +387,13 @@
 def shards(spectra, station_ids, counts):
     row_count = lax.axis_size("row")
     column_count = lax.axis_size("col")
-    readers = row_count * column_count
     slot_count, segments, _ = spectra.shape
     home_rows = slot_count // 2
-    packed = whiten_pack(spectra, station_ids, counts, readers)
-    received = lax.all_to_all(packed, ("row", "col"), split_axis=0, concat_axis=0, tiled=True)
+    packed = whiten_pack(spectra, station_ids, counts, row_count, column_count)
+    order = [r * column_count + 2 * h + k for k in range(2) for h in range(column_count // 2) for r in range(row_count)]
+    received = lax.all_to_all(
+        packed, ("row", "col"), split_axis=0, concat_axis=0, tiled=True, axis_index_groups=[order]
+    )
     white = settle(received, home_rows, segments)
     row_blocks = gather_rows(white, column_count)
     col_blocks = gather_columns(white, row_count)

time: 53.2 us -> 52.2 us (0.981)
  starting transfers between devices: 5.73 us -> 4.94 us
  waiting for transfers between devices: 9.74 us -> 9.1 us
    ppermute x10, starting transfers between devices: 5.73 us -> 4.94 us  [across(): return lax.ppermute(value, axis, [(i, i ^ distance) for i in range(size)])]
    ppermute x10, waiting for transfers between devices: 9.74 us -> 9.1 us  [across(): return lax.ppermute(value, axis, [(i, i ^ distance) for i in range(size)])]
  transfers between devices with their start and end apart: 10 -> 10, of which waited for: 5 -> 6; matrix products, arithmetic and copies ran while one was open for 0% -> 0% of each run, Pallas kernels for 4% -> 4%
where the time goes in v5:
time: 52.2 us; the launch traced here: 52.1 us
  blocking collectives  20.7 us (40%)
  Pallas kernels  15.9 us (30%)
  waiting for transfers between devices  9.1 us (17%)
  starting transfers between devices  4.94 us (9%)
  between operations  0.73 us (1%)
  local copies, waits for them, and re-layouts  0.67 us (1%)
    all_to_all x1, blocking collectives, shards(): lax.all_to_all(packed, ('row', 'col'), split_axis=0, concat_axis=0, tiled...  20.7 us
    ppermute x10, waiting for transfers between devices, across(): return lax.ppermute(value, axis, [(i, i ^ distance) for i in range(size)])  9.1 us
    pallas_call x1, Pallas kernels, whiten_pack(): pl.pallas_call(functools.partial(whiten_kernel, home_rows, row_count, col...  6.79 us
    pallas_call x1, Pallas kernels, pair_tiles(): pl.pallas_call(functools.partial(pair_kernel, segments, col_n), in_specs=...  6.26 us
    ppermute x10, starting transfers between devices, across(): return lax.ppermute(value, axis, [(i, i ^ distance) for i in range(size)])  4.94 us
    pallas_call x1, Pallas kernels, prepare_rows(): pl.pallas_call(functools.partial(rows_kernel, segments, row_n), out_shape...  2.3 us
  transfers between devices with their start and end apart: 10, of which 6 were waited for; matrix products, arithmetic and copies ran while one was open for 0% of the time, Pallas kernels for 4%

profile of v5, /device:TPU:0, one launch (start us, length us, event | category | flops | bytes accessed | tf_op | source)
XLA Modules:
  0.0 52.1 jit_solution(2961144158179423623)
XLA Ops:
  0.7 0.7 %copy-done = s32[192]{0:T(256)S(1)} copy-done((s32[192]{0:T(256)S(1)}, s32[192]{0:T(256)}, u32[]{:S(2)}) %copy-start) | copy-done | bytes 792
  1.3 6.8 %whiten_pack.1 = s16[256,768]{1,0:T(8,128)(2,1)S(1)} custom-call(s32[1]{0:T(128)S(6)} %copy.4.count_ref, s32[1,192]{1,0:T(1,128)S(1)} %bitcast.5, bf16[192,144,128]{2,1,0:T(8,128)(2,1)} %source_ref.1), custom_call_target="tpu_custom_call" | custom-call | tf_op jit(solution)/shard_map/whiten_pack/pallas_call | solution.py:166
  8.1 20.7 %all_to_all.11 = s16[32,8,768]{2,1,0:T(8,128)(2,1)S(1)} all-to-all(s16[32,8,768]{2,1,0:T(8,128)(2,1)S(1)} %bitcast.3), channel_id=1, replica_groups={{0,8,16,24,2,10,18,26,4,12,20,28,6,14,22,30,1,9,17,25,3,11,19,27,5,13,2..., dimensions={0} | all-to-all | bytes 786432 | tf_op jit(solution)/shard_map/all_to_all | solution.py:394
  28.9 0.5 settle.1.refs_0_
  29.4 0.9 %collective-permute-start.1 = (s16[96,896]{1,0:T(8,128)(2,1)S(1)}, s16[96,896]{1,0:T(8,128)(2,1)S(1)}, u32[]{:S(2)}, u32[]{:S(2)}) collective-permute-start(s16[96,896]{1,0:T(8,128)(2,1)S(1)} %settle.1.refs_0_), channel_id=1, source_target_pairs={{0,2},{1,3},{2,0},{3,1},{4,6},{5,7},{6,4},{7,5},{8,10},{9,11},{10,... | collective-permute-start | bytes 516104 | tf_op jit(solution)/shard_map/ppermute | solution.py:362
  30.2 0.2 collective-permute-start.8
  30.4 1.8 %collective-permute-start.7 = (s16[96,896]{1,0:T(8,128)(2,1)S(1)}, s16[96,896]{1,0:T(8,128)(2,1)S(1)}, u32[]{:S(2)}, u32[]{:S(2)}) collective-permute-start(s16[96,896]{1,0:T(8,128)(2,1)S(1)} %settle.1.refs_0_), channel_id=1, source_target_pairs={{0,8},{8,0},{16,24},{24,16},{1,9},{9,1},{17,25},{25,17},{2,10},{10... | collective-permute-start | bytes 516104 | tf_op jit(solution)/shard_map/ppermute | solution.py:362
  32.2 0.2 collective-permute-start.3
  32.4 0.0 collective-permute-start
  32.4 2.4 %collective-permute-done.1.refs_2_ = s16[96,896]{1,0:T(8,128)(2,1)S(1)} collective-permute-done((s16[96,896]{1,0:T(8,128)(2,1)S(1)}, s16[96,896]{1,0:T(8,128)(2,1)S(1)}, u32[]{:S(2)}, u32[]{:S(2)}) %collective-permute-start.1) | collective-permute-done | bytes 172064 | tf_op jit(solution)/shard_map/ppermute | solution.py:362
  34.8 1.2 %collective-permute-start.5 = (s16[96,896]{1,0:T(8,128)(2,1)S(1)}, s16[96,896]{1,0:T(8,128)(2,1)S(1)}, u32[]{:S(2)}, u32[]{:S(2)}) collective-permute-start(s16[96,896]{1,0:T(8,128)(2,1)S(1)} %collective-permute-done.1.refs_2_), channel_id=1, source_target_pairs={{0,4},{1,5},{2,6},{3,7},{4,0},{5,1},{6,2},{7,3},{8,12},{9,13},{10,... | collective-permute-start | bytes 516104 | tf_op jit(solution)/shard_map/ppermute | solution.py:362
  36.1 4.0 %collective-permute-done.8.in_ref.refs_2_ = s16[96,896]{1,0:T(8,128)(2,1)S(1)} collective-permute-done((s16[96,896]{1,0:T(8,128)(2,1)S(1)}, s16[96,896]{1,0:T(8,128)(2,1)S(1)}, u32[]{:S(2)}, u32[]{:S(2)}) %collective-permute-start.8) | collective-permute-done | bytes 172064 | tf_op jit(solution)/shard_map/ppermute | solution.py:362
  40.0 0.1 collective-permute-start.9
  40.1 0.0 collective-permute-done.3.refs_4_
  40.1 0.1 collective-permute-start.2
  40.2 0.0 collective-permute-done.refs_1_
  40.2 0.5 collective-permute-start.4
  40.7 0.4 collective-permute-done.5.refs_6_
  41.2 0.7 %collective-permute-done.4.refs_5_ = s16[96,896]{1,0:T(8,128)(2,1)S(1)} collective-permute-done((s16[96,896]{1,0:T(8,128)(2,1)S(1)}, s16[96,896]{1,0:T(8,128)(2,1)S(1)}, u32[]{:S(2)}, u32[]{:S(2)}) %collective-permute-start.4) | collective-permute-done | bytes 172064 | tf_op jit(solution)/shard_map/ppermute | solution.py:362
  41.9 0.0 collective-permute-done.2.refs_3_
  41.9 0.7 %collective-permute-done.6.refs_7_ = s16[96,896]{1,0:T(8,128)(2,1)S(1)} collective-permute-done((s16[96,896]{1,0:T(8,128)(2,1)S(1)}, s16[96,896]{1,0:T(8,128)(2,1)S(1)}, u32[]{:S(2)}, u32[]{:S(2)}) %collective-permute-start.6) | collective-permute-done | bytes 172064 | tf_op jit(solution)/shard_map/ppermute | solution.py:362
  42.6 2.3 %prepare_rows.1 = (bf16[3,768,896]{2,1,0:T(8,128)(2,1)S(1)}, f32[768,128]{1,0:T(8,128)S(1)}) custom-call(s32[2,8]{1,0:T(2,128)S(1)} %pad_add_fusion.place_ref, s16[96,896]{1,0:T(8,128)(2,1)S(1)} %settle.1.refs_0_, s16[96,896]{1,0:T(8,128)(2,1)S(1)} %collective-permute-done.refs_1_, s16[96,896]{1,0:T(8,128)(2,1)S(1)} %collective-permute-done.1.refs_2_, ...), custom_call_target="tpu_custom_call" | custom-call | flops 1 | bytes 1 | tf_op jit(solution)/shard_map/prepare_rows/pallas_call | solution.py:306
  44.9 0.9 %collective-permute-done.9.refs_3_ = s16[96,896]{1,0:T(8,128)(2,1)S(1)} collective-permute-done((s16[96,896]{1,0:T(8,128)(2,1)S(1)}, s16[96,896]{1,0:T(8,128)(2,1)S(1)}, u32[]{:S(2)}, u32[]{:S(2)}) %collective-permute-start.9) | collective-permute-done | bytes 172064 | tf_op jit(solution)/shard_map/ppermute | solution.py:362
  45.8 6.3 %pair_tiles.1 = bf16[3,2,768,384]{3,2,1,0:T(8,128)(2,1)} custom-call(s32[2,8]{1,0:T(2,128)S(1)} %pad_add_fusion.place_ref, bf16[3,768,896]{2,1,0:T(8,128)(2,1)S(1)} %get-tuple-element.7.a_ref, f32[768,128]{1,0:T(8,128)S(1)} %get-tuple-element.8.scale_ref, s16[96,896]{1,0:T(8,128)(2,1)S(1)} %settle.1.refs_0_, ...), custom_call_target="tpu_custom_call" | custom-call | tf_op jit(solution)/shard_map/pair_tiles/pallas_call | solution.py:325
  (6 shorter events, 0.0 us)
Async XLA Ops:
  0.7 0.7 %copy-start = (s32[192]{0:T(256)S(1)}, s32[192]{0:T(256)}, u32[]{:S(2)}) copy-start(s32[192]{0:T(256)} %param.4) | copy-start | bytes 2308
  29.4 5.5 %collective-permute-start.1 = (s16[96,896]{1,0:T(8,128)(2,1)S(1)}, s16[96,896]{1,0:T(8,128)(2,1)S(1)}, u32[]{:S(2)}, u32[]{:S(2)}) collective-permute-start(s16[96,896]{1,0:T(8,128)(2,1)S(1)} %settle.1.refs_0_), channel_id=1, source_target_pairs={{0,2},{1,3},{2,0},{3,1},{4,6},{5,7},{6,4},{7,5},{8,10},{9,11},{10,... | collective-permute-start | bytes 516104 | tf_op jit(solution)/shard_map/ppermute | solution.py:362
  30.2 9.8 %collective-permute-start.8 = (s16[96,896]{1,0:T(8,128)(2,1)S(1)}, s16[96,896]{1,0:T(8,128)(2,1)S(1)}, u32[]{:S(2)}, u32[]{:S(2)}) collective-permute-start(s16[96,896]{1,0:T(8,128)(2,1)S(1)} %settle.1.refs_0_), channel_id=1, source_target_pairs={{0,16},{8,24},{16,0},{24,8},{1,17},{9,25},{17,1},{25,9},{2,18},{10... | collective-permute-start | bytes 516104 | tf_op jit(solution)/shard_map/ppermute | solution.py:362
  30.4 14.5 %collective-permute-start.7 = (s16[96,896]{1,0:T(8,128)(2,1)S(1)}, s16[96,896]{1,0:T(8,128)(2,1)S(1)}, u32[]{:S(2)}, u32[]{:S(2)}) collective-permute-start(s16[96,896]{1,0:T(8,128)(2,1)S(1)} %settle.1.refs_0_), channel_id=1, source_target_pairs={{0,8},{8,0},{16,24},{24,16},{1,9},{9,1},{17,25},{25,17},{2,10},{10... | collective-permute-start | bytes 516104 | tf_op jit(solution)/shard_map/ppermute | solution.py:362
  32.2 7.9 %collective-permute-start.3 = (s16[96,896]{1,0:T(8,128)(2,1)S(1)}, s16[96,896]{1,0:T(8,128)(2,1)S(1)}, u32[]{:S(2)}, u32[]{:S(2)}) collective-permute-start(s16[96,896]{1,0:T(8,128)(2,1)S(1)} %settle.1.refs_0_), channel_id=1, source_target_pairs={{0,4},{1,5},{2,6},{3,7},{4,0},{5,1},{6,2},{7,3},{8,12},{9,13},{10,... | collective-permute-start | bytes 516104 | tf_op jit(solution)/shard_map/ppermute | solution.py:362
  32.4 7.8 %collective-permute-start = (s16[96,896]{1,0:T(8,128)(2,1)S(1)}, s16[96,896]{1,0:T(8,128)(2,1)S(1)}, u32[]{:S(2)}, u32[]{:S(2)}) collective-permute-start(s16[96,896]{1,0:T(8,128)(2,1)S(1)} %settle.1.refs_0_), channel_id=1, source_target_pairs={{0,1},{1,0},{2,3},{3,2},{4,5},{5,4},{6,7},{7,6},{8,9},{9,8},{10,11... | collective-permute-start | bytes 516104 | tf_op jit(solution)/shard_map/ppermute | solution.py:362
  34.8 6.3 %collective-permute-start.5 = (s16[96,896]{1,0:T(8,128)(2,1)S(1)}, s16[96,896]{1,0:T(8,128)(2,1)S(1)}, u32[]{:S(2)}, u32[]{:S(2)}) collective-permute-start(s16[96,896]{1,0:T(8,128)(2,1)S(1)} %collective-permute-done.1.refs_2_), channel_id=1, source_target_pairs={{0,4},{1,5},{2,6},{3,7},{4,0},{5,1},{6,2},{7,3},{8,12},{9,13},{10,... | collective-permute-start | bytes 516104 | tf_op jit(solution)/shard_map/ppermute | solution.py:362
  40.0 5.7 %collective-permute-start.9 = (s16[96,896]{1,0:T(8,128)(2,1)S(1)}, s16[96,896]{1,0:T(8,128)(2,1)S(1)}, u32[]{:S(2)}, u32[]{:S(2)}) collective-permute-start(s16[96,896]{1,0:T(8,128)(2,1)S(1)} %copy_block.1), channel_id=1, source_target_pairs={{0,8},{8,0},{16,24},{24,16},{1,9},{9,1},{17,25},{25,17},{2,10},{10... | collective-permute-start | bytes 516104 | tf_op jit(solution)/shard_map/ppermute | solution.py:362
  40.1 1.7 %collective-permute-start.2 = (s16[96,896]{1,0:T(8,128)(2,1)S(1)}, s16[96,896]{1,0:T(8,128)(2,1)S(1)}, u32[]{:S(2)}, u32[]{:S(2)}) collective-permute-start(s16[96,896]{1,0:T(8,128)(2,1)S(1)} %collective-permute-done.1.refs_2_), channel_id=1, source_target_pairs={{0,1},{1,0},{2,3},{3,2},{4,5},{5,4},{6,7},{7,6},{8,9},{9,8},{10,11... | collective-permute-start | bytes 516104 | tf_op jit(solution)/shard_map/ppermute | solution.py:362
  40.2 1.6 %collective-permute-start.4 = (s16[96,896]{1,0:T(8,128)(2,1)S(1)}, s16[96,896]{1,0:T(8,128)(2,1)S(1)}, u32[]{:S(2)}, u32[]{:S(2)}) collective-permute-start(s16[96,896]{1,0:T(8,128)(2,1)S(1)} %collective-permute-done.3.refs_4_), channel_id=1, source_target_pairs={{0,1},{1,0},{2,3},{3,2},{4,5},{5,4},{6,7},{7,6},{8,9},{9,8},{10,11... | collective-permute-start | bytes 516104 | tf_op jit(solution)/shard_map/ppermute | solution.py:362
  41.2 1.4 %collective-permute-start.6 = (s16[96,896]{1,0:T(8,128)(2,1)S(1)}, s16[96,896]{1,0:T(8,128)(2,1)S(1)}, u32[]{:S(2)}, u32[]{:S(2)}) collective-permute-start(s16[96,896]{1,0:T(8,128)(2,1)S(1)} %collective-permute-done.5.refs_6_), channel_id=1, source_target_pairs={{0,1},{1,0},{2,3},{3,2},{4,5},{5,4},{6,7},{7,6},{8,9},{9,8},{10,11... | collective-permute-start | bytes 516104 | tf_op jit(solution)/shard_map/ppermute | solution.py:362

commit v6 on v5

--- a/solution.py
+++ b/solution.py
@@ -93,7 +93,7 @@
     column_of = target - row_of * column_count
     half_of = jnp.floor((column_of + 0.5) * 0.5)
     core_of = column_of - 2.0 * half_of
-    peer = (core_of * (column_count // 2) + half_of) * row_count + row_of
+    peer = (core_of * row_count + row_of) * (column_count // 2) + half_of
     place = jnp.where(live, peer * slab + within, -1.0)
     send_rows = out_ref.shape[0]
     spot = iota((send_rows, slot_count), 0).astype(jnp.float32)
@@ -390,7 +390,7 @@
     slot_count, segments, _ = spectra.shape
     home_rows = slot_count // 2
     packed = whiten_pack(spectra, station_ids, counts, row_count, column_count)
-    order = [r * column_count + 2 * h + k for k in range(2) for h in range(column_count // 2) for r in range(row_count)]
+    order = [r * column_count + 2 * h + k for k in range(2) for r in range(row_count) for h in range(column_count // 2)]
     received = lax.all_to_all(
         packed, ("row", "col"), split_axis=0, concat_axis=0, tiled=True, axis_index_groups=[order]
     )

time: 52.2 us -> 52.8 us (1.011)
  waiting for transfers between devices: 9.1 us -> 10.4 us
  starting transfers between devices: 4.94 us -> 3.77 us
    ppermute x10, waiting for transfers between devices: 9.1 us -> 10.4 us  [across(): return lax.ppermute(value, axis, [(i, i ^ distance) for i in range(size)])]
    ppermute x10, starting transfers between devices: 4.94 us -> 3.77 us  [across(): return lax.ppermute(value, axis, [(i, i ^ distance) for i in range(size)])]
where the time goes in v6:
time: 52.8 us; the launch traced here: 52.6 us
  blocking collectives  21.1 us (40%)
  Pallas kernels  15.9 us (30%)
  waiting for transfers between devices  10.4 us (20%)
  starting transfers between devices  3.77 us (7%)
  between operations  0.73 us (1%)
  local copies, waits for them, and re-layouts  0.67 us (1%)
    all_to_all x1, blocking collectives, shards(): lax.all_to_all(packed, ('row', 'col'), split_axis=0, concat_axis=0, tiled...  21.1 us
    ppermute x10, waiting for transfers between devices, across(): return lax.ppermute(value, axis, [(i, i ^ distance) for i in range(size)])  10.4 us
    pallas_call x1, Pallas kernels, whiten_pack(): pl.pallas_call(functools.partial(whiten_kernel, home_rows, row_count, col...  6.79 us
    pallas_call x1, Pallas kernels, pair_tiles(): pl.pallas_call(functools.partial(pair_kernel, segments, col_n), in_specs=...  6.28 us
    ppermute x10, starting transfers between devices, across(): return lax.ppermute(value, axis, [(i, i ^ distance) for i in range(size)])  3.77 us
    pallas_call x1, Pallas kernels, prepare_rows(): pl.pallas_call(functools.partial(rows_kernel, segments, row_n), out_shape...  2.3 us
  transfers between devices with their start and end apart: 10, of which 6 were waited for; matrix products, arithmetic and copies ran while one was open for 0% of the time, Pallas kernels for 4%

profile of v6, /device:TPU:0, one launch (start us, length us, event | category | flops | bytes accessed | tf_op | source)
XLA Modules:
  0.0 52.6 jit_solution(12759473935259490524)
XLA Ops:
  0.7 0.7 %copy-done = s32[192]{0:T(256)S(1)} copy-done((s32[192]{0:T(256)S(1)}, s32[192]{0:T(256)}, u32[]{:S(2)}) %copy-start) | copy-done | bytes 792
  1.3 6.8 %whiten_pack.1 = s16[256,768]{1,0:T(8,128)(2,1)S(1)} custom-call(s32[1]{0:T(128)S(6)} %copy.4.count_ref, s32[1,192]{1,0:T(1,128)S(1)} %bitcast.5, bf16[192,144,128]{2,1,0:T(8,128)(2,1)} %source_ref.1), custom_call_target="tpu_custom_call" | custom-call | tf_op jit(solution)/shard_map/whiten_pack/pallas_call | solution.py:166
  8.1 21.1 %all_to_all.11 = s16[32,8,768]{2,1,0:T(8,128)(2,1)S(1)} all-to-all(s16[32,8,768]{2,1,0:T(8,128)(2,1)S(1)} %bitcast.3), channel_id=1, replica_groups={{0,2,4,6,8,10,12,14,16,18,20,22,24,26,28,30,1,3,5,7,9,11,13,15,17,19,21..., dimensions={0} | all-to-all | bytes 786432 | tf_op jit(solution)/shard_map/all_to_all | solution.py:394
  29.3 0.5 settle.1.refs_0_
  29.8 0.2 collective-permute-start.1
  30.0 0.9 %collective-permute-start.8 = (s16[96,896]{1,0:T(8,128)(2,1)S(1)}, s16[96,896]{1,0:T(8,128)(2,1)S(1)}, u32[]{:S(2)}, u32[]{:S(2)}) collective-permute-start(s16[96,896]{1,0:T(8,128)(2,1)S(1)} %settle.1.refs_0_), channel_id=1, source_target_pairs={{0,16},{8,24},{16,0},{24,8},{1,17},{9,25},{17,1},{25,9},{2,18},{10... | collective-permute-start | bytes 516104 | tf_op jit(solution)/shard_map/ppermute | solution.py:362
  30.9 0.6 %collective-permute-start.7 = (s16[96,896]{1,0:T(8,128)(2,1)S(1)}, s16[96,896]{1,0:T(8,128)(2,1)S(1)}, u32[]{:S(2)}, u32[]{:S(2)}) collective-permute-start(s16[96,896]{1,0:T(8,128)(2,1)S(1)} %settle.1.refs_0_), channel_id=1, source_target_pairs={{0,8},{8,0},{16,24},{24,16},{1,9},{9,1},{17,25},{25,17},{2,10},{10... | collective-permute-start | bytes 516104 | tf_op jit(solution)/shard_map/ppermute | solution.py:362
  31.5 1.1 %collective-permute-start.3 = (s16[96,896]{1,0:T(8,128)(2,1)S(1)}, s16[96,896]{1,0:T(8,128)(2,1)S(1)}, u32[]{:S(2)}, u32[]{:S(2)}) collective-permute-start(s16[96,896]{1,0:T(8,128)(2,1)S(1)} %settle.1.refs_0_), channel_id=1, source_target_pairs={{0,4},{1,5},{2,6},{3,7},{4,0},{5,1},{6,2},{7,3},{8,12},{9,13},{10,... | collective-permute-start | bytes 516104 | tf_op jit(solution)/shard_map/ppermute | solution.py:362
  32.5 0.0 collective-permute-start
  32.6 3.0 %collective-permute-done.1.refs_2_ = s16[96,896]{1,0:T(8,128)(2,1)S(1)} collective-permute-done((s16[96,896]{1,0:T(8,128)(2,1)S(1)}, s16[96,896]{1,0:T(8,128)(2,1)S(1)}, u32[]{:S(2)}, u32[]{:S(2)}) %collective-permute-start.1) | collective-permute-done | bytes 172064 | tf_op jit(solution)/shard_map/ppermute | solution.py:362
  35.5 0.3 collective-permute-start.5
  35.9 4.1 %collective-permute-done.8.in_ref.refs_2_ = s16[96,896]{1,0:T(8,128)(2,1)S(1)} collective-permute-done((s16[96,896]{1,0:T(8,128)(2,1)S(1)}, s16[96,896]{1,0:T(8,128)(2,1)S(1)}, u32[]{:S(2)}, u32[]{:S(2)}) %collective-permute-start.8) | collective-permute-done | bytes 172064 | tf_op jit(solution)/shard_map/ppermute | solution.py:362
  40.0 0.1 collective-permute-start.9
  40.1 0.1 collective-permute-start.2
  40.2 0.0 collective-permute-done.refs_1_
  40.2 0.5 collective-permute-start.4
  40.7 0.3 collective-permute-done.5.refs_6_
  41.0 0.0 collective-permute-start.6
  41.0 0.8 %collective-permute-done.4.refs_5_ = s16[96,896]{1,0:T(8,128)(2,1)S(1)} collective-permute-done((s16[96,896]{1,0:T(8,128)(2,1)S(1)}, s16[96,896]{1,0:T(8,128)(2,1)S(1)}, u32[]{:S(2)}, u32[]{:S(2)}) %collective-permute-start.4) | collective-permute-done | bytes 172064 | tf_op jit(solution)/shard_map/ppermute | solution.py:362
  41.8 0.0 collective-permute-done.2.refs_3_
  41.8 0.6 %collective-permute-done.6.refs_7_ = s16[96,896]{1,0:T(8,128)(2,1)S(1)} collective-permute-done((s16[96,896]{1,0:T(8,128)(2,1)S(1)}, s16[96,896]{1,0:T(8,128)(2,1)S(1)}, u32[]{:S(2)}, u32[]{:S(2)}) %collective-permute-start.6) | collective-permute-done | bytes 172064 | tf_op jit(solution)/shard_map/ppermute | solution.py:362
  42.4 2.3 %prepare_rows.1 = (bf16[3,768,896]{2,1,0:T(8,128)(2,1)S(1)}, f32[768,128]{1,0:T(8,128)S(1)}) custom-call(s32[2,8]{1,0:T(2,128)S(1)} %pad_add_fusion.place_ref, s16[96,896]{1,0:T(8,128)(2,1)S(1)} %settle.1.refs_0_, s16[96,896]{1,0:T(8,128)(2,1)S(1)} %collective-permute-done.refs_1_, s16[96,896]{1,0:T(8,128)(2,1)S(1)} %collective-permute-done.1.refs_2_, ...), custom_call_target="tpu_custom_call" | custom-call | flops 1 | bytes 1 | tf_op jit(solution)/shard_map/prepare_rows/pallas_call | solution.py:306
  44.7 1.6 %collective-permute-done.9.refs_3_ = s16[96,896]{1,0:T(8,128)(2,1)S(1)} collective-permute-done((s16[96,896]{1,0:T(8,128)(2,1)S(1)}, s16[96,896]{1,0:T(8,128)(2,1)S(1)}, u32[]{:S(2)}, u32[]{:S(2)}) %collective-permute-start.9) | collective-permute-done | bytes 172064 | tf_op jit(solution)/shard_map/ppermute | solution.py:362
  46.3 6.3 %pair_tiles.1 = bf16[3,2,768,384]{3,2,1,0:T(8,128)(2,1)} custom-call(s32[2,8]{1,0:T(2,128)S(1)} %pad_add_fusion.place_ref, bf16[3,768,896]{2,1,0:T(8,128)(2,1)S(1)} %get-tuple-element.7.a_ref, f32[768,128]{1,0:T(8,128)S(1)} %get-tuple-element.8.scale_ref, s16[96,896]{1,0:T(8,128)(2,1)S(1)} %settle.1.refs_0_, ...), custom_call_target="tpu_custom_call" | custom-call | tf_op jit(solution)/shard_map/pair_tiles/pallas_call | solution.py:325
  (6 shorter events, 0.0 us)
Async XLA Ops:
  0.7 0.7 %copy-start = (s32[192]{0:T(256)S(1)}, s32[192]{0:T(256)}, u32[]{:S(2)}) copy-start(s32[192]{0:T(256)} %param.4) | copy-start | bytes 2308
  29.8 5.8 %collective-permute-start.1 = (s16[96,896]{1,0:T(8,128)(2,1)S(1)}, s16[96,896]{1,0:T(8,128)(2,1)S(1)}, u32[]{:S(2)}, u32[]{:S(2)}) collective-permute-start(s16[96,896]{1,0:T(8,128)(2,1)S(1)} %settle.1.refs_0_), channel_id=1, source_target_pairs={{0,2},{1,3},{2,0},{3,1},{4,6},{5,7},{6,4},{7,5},{8,10},{9,11},{10,... | collective-permute-start | bytes 516104 | tf_op jit(solution)/shard_map/ppermute | solution.py:362
  30.0 10.0 %collective-permute-start.8 = (s16[96,896]{1,0:T(8,128)(2,1)S(1)}, s16[96,896]{1,0:T(8,128)(2,1)S(1)}, u32[]{:S(2)}, u32[]{:S(2)}) collective-permute-start(s16[96,896]{1,0:T(8,128)(2,1)S(1)} %settle.1.refs_0_), channel_id=1, source_target_pairs={{0,16},{8,24},{16,0},{24,8},{1,17},{9,25},{17,1},{25,9},{2,18},{10... | collective-permute-start | bytes 516104 | tf_op jit(solution)/shard_map/ppermute | solution.py:362
  30.9 13.8 %collective-permute-start.7 = (s16[96,896]{1,0:T(8,128)(2,1)S(1)}, s16[96,896]{1,0:T(8,128)(2,1)S(1)}, u32[]{:S(2)}, u32[]{:S(2)}) collective-permute-start(s16[96,896]{1,0:T(8,128)(2,1)S(1)} %settle.1.refs_0_), channel_id=1, source_target_pairs={{0,8},{8,0},{16,24},{24,16},{1,9},{9,1},{17,25},{25,17},{2,10},{10... | collective-permute-start | bytes 516104 | tf_op jit(solution)/shard_map/ppermute | solution.py:362
  31.5 8.6 %collective-permute-start.3 = (s16[96,896]{1,0:T(8,128)(2,1)S(1)}, s16[96,896]{1,0:T(8,128)(2,1)S(1)}, u32[]{:S(2)}, u32[]{:S(2)}) collective-permute-start(s16[96,896]{1,0:T(8,128)(2,1)S(1)} %settle.1.refs_0_), channel_id=1, source_target_pairs={{0,4},{1,5},{2,6},{3,7},{4,0},{5,1},{6,2},{7,3},{8,12},{9,13},{10,... | collective-permute-start | bytes 516104 | tf_op jit(solution)/shard_map/ppermute | solution.py:362
  32.5 7.6 %collective-permute-start = (s16[96,896]{1,0:T(8,128)(2,1)S(1)}, s16[96,896]{1,0:T(8,128)(2,1)S(1)}, u32[]{:S(2)}, u32[]{:S(2)}) collective-permute-start(s16[96,896]{1,0:T(8,128)(2,1)S(1)} %settle.1.refs_0_), channel_id=1, source_target_pairs={{0,1},{1,0},{2,3},{3,2},{4,5},{5,4},{6,7},{7,6},{8,9},{9,8},{10,11... | collective-permute-start | bytes 516104 | tf_op jit(solution)/shard_map/ppermute | solution.py:362
  35.5 5.5 %collective-permute-start.5 = (s16[96,896]{1,0:T(8,128)(2,1)S(1)}, s16[96,896]{1,0:T(8,128)(2,1)S(1)}, u32[]{:S(2)}, u32[]{:S(2)}) collective-permute-start(s16[96,896]{1,0:T(8,128)(2,1)S(1)} %collective-permute-done.1.refs_2_), channel_id=1, source_target_pairs={{0,4},{1,5},{2,6},{3,7},{4,0},{5,1},{6,2},{7,3},{8,12},{9,13},{10,... | collective-permute-start | bytes 516104 | tf_op jit(solution)/shard_map/ppermute | solution.py:362
  40.0 6.3 %collective-permute-start.9 = (s16[96,896]{1,0:T(8,128)(2,1)S(1)}, s16[96,896]{1,0:T(8,128)(2,1)S(1)}, u32[]{:S(2)}, u32[]{:S(2)}) collective-permute-start(s16[96,896]{1,0:T(8,128)(2,1)S(1)} %copy_block.1), channel_id=1, source_target_pairs={{0,8},{8,0},{16,24},{24,16},{1,9},{9,1},{17,25},{25,17},{2,10},{10... | collective-permute-start | bytes 516104 | tf_op jit(solution)/shard_map/ppermute | solution.py:362
  40.1 1.7 %collective-permute-start.2 = (s16[96,896]{1,0:T(8,128)(2,1)S(1)}, s16[96,896]{1,0:T(8,128)(2,1)S(1)}, u32[]{:S(2)}, u32[]{:S(2)}) collective-permute-start(s16[96,896]{1,0:T(8,128)(2,1)S(1)} %collective-permute-done.1.refs_2_), channel_id=1, source_target_pairs={{0,1},{1,0},{2,3},{3,2},{4,5},{5,4},{6,7},{7,6},{8,9},{9,8},{10,11... | collective-permute-start | bytes 516104 | tf_op jit(solution)/shard_map/ppermute | solution.py:362
  40.2 1.6 %collective-permute-start.4 = (s16[96,896]{1,0:T(8,128)(2,1)S(1)}, s16[96,896]{1,0:T(8,128)(2,1)S(1)}, u32[]{:S(2)}, u32[]{:S(2)}) collective-permute-start(s16[96,896]{1,0:T(8,128)(2,1)S(1)} %collective-permute-done.3.refs_4_), channel_id=1, source_target_pairs={{0,1},{1,0},{2,3},{3,2},{4,5},{5,4},{6,7},{7,6},{8,9},{9,8},{10,11... | collective-permute-start | bytes 516104 | tf_op jit(solution)/shard_map/ppermute | solution.py:362
  41.0 1.4 %collective-permute-start.6 = (s16[96,896]{1,0:T(8,128)(2,1)S(1)}, s16[96,896]{1,0:T(8,128)(2,1)S(1)}, u32[]{:S(2)}, u32[]{:S(2)}) collective-permute-start(s16[96,896]{1,0:T(8,128)(2,1)S(1)} %collective-permute-done.5.refs_6_), channel_id=1, source_target_pairs={{0,1},{1,0},{2,3},{3,2},{4,5},{5,4},{6,7},{7,6},{8,9},{9,8},{10,11... | collective-permute-start | bytes 516104 | tf_op jit(solution)/shard_map/ppermute | solution.py:362
